TPU v7x, 256 devices: a whole 4x4x8 slice. The times are simulated.
256 devices in a mesh: seq: 64 (over z, y, core), tp: 4 (over x).
Axes of the slice: x: 4, y: 4, z: 8, core: 2. Of those that a mesh axis runs over, the one named last changes fastest.
Arguments:
- query: bfloat16 [53248, 2048], P('seq', 'tp'), may hold values from -200 to 200
- d_attended: bfloat16 [53248, 2048], P('seq', 'tp'), may hold values from -6 to 6
- encoded: bfloat16 [1024, 128, 896], P('seq', 'tp'), may hold values from -6 to 6
- key_weight: bfloat16 [896, 2048], replicated, may hold values from -0.1875 to 0.1875
- value_weight: bfloat16 [896, 2048], replicated, may hold values from -0.1875 to 0.1875
- nbr_shard: int32 [832, 2], P('seq'), may hold values from 0 to 63, all different within a row; in each aligned block of 13 rows (0 to 12, 13 to 25, ...) at most 2 rows name the same one
- nbr_row: int32 [832, 2], P('seq'), may hold values from 0 to 15
Outputs:
- attended: bfloat16 [53248, 2048], P('seq', 'tp')
- d_query: bfloat16 [53248, 2048], P('seq', 'tp')
- d_encoded: bfloat16 [1024, 128, 896], P('seq', 'tp')
Inputs may be any that keep to these rules, and one draw needn't show every extreme that they name: `nbr_shard`: a span's 2 neighbours lie on different indices; among the 13 spans of one sequence no index is named more than 2 times, a bound that some block reaches.
All inputs are finite; a program needn't handle non-finite values.
Results may differ from a plain program's by a relative error of at most 0.017.
The roundings to bfloat16 on the way count: a program that leaves them out, or rounds other values in their place, can miss the bound.
Values may be sent and summed in bfloat16 or wider, within the bound.
No kernel may reach another device: no remote copies, remote signals or barrier semaphores. Data moves between devices by JAX's collectives and lax.ppermute only.
A program may use at most 192 MiB of HBM per device.

v0:
```python
import jax
import jax.numpy as jnp
from jax import lax
from jax.sharding import PartitionSpec as P

HD = 128
SPAN = 64


def shift_rows(tokens_in):
    padding = jnp.zeros((SPAN - 1, tokens_in.shape[1]), tokens_in.dtype)
    return jnp.concatenate([tokens_in[SPAN - 1 :], padding], 0)


def unshift_rows(tokens_in):
    padding = jnp.zeros((SPAN - 1, tokens_in.shape[1]), tokens_in.dtype)
    return jnp.concatenate([padding, tokens_in[: tokens_in.shape[0] - SPAN + 1]], 0)


def attend(shifted, grad_shift, key_rows, value_rows):
    factor = HD ** (-0.5)
    f32 = jnp.float32
    scores = jnp.einsum("cqhd,ckhd->chqk", shifted, key_rows, preferred_element_type=f32) * factor
    row_max = jnp.max(scores, axis=-1, keepdims=True)
    weights = jnp.exp(scores - row_max)
    probs = weights / jnp.sum(weights, axis=-1, keepdims=True)
    probs_b = probs.astype(jnp.bfloat16)
    blended = jnp.einsum("chqk,ckhd->cqhd", probs_b, value_rows, preferred_element_type=f32)
    grad_probs = jnp.einsum("cqhd,ckhd->chqk", grad_shift, value_rows, preferred_element_type=f32)
    inner = jnp.sum(probs * grad_probs, axis=-1, keepdims=True)
    grad_scores = (probs * (grad_probs - inner) * factor).astype(jnp.bfloat16)
    grad_shifted = jnp.einsum("chqk,ckhd->cqhd", grad_scores, key_rows, preferred_element_type=f32)
    grad_keys = jnp.einsum(
        "chqk,cqhd->ckhd", grad_scores, shifted, preferred_element_type=f32
    ).astype(jnp.bfloat16)
    grad_values = jnp.einsum(
        "chqk,cqhd->ckhd", probs_b, grad_shift, preferred_element_type=f32
    ).astype(jnp.bfloat16)
    return (blended, grad_shifted, grad_keys, grad_values)


def shards(query, d_attended, encoded, key_weight, value_weight, nbr_shard, nbr_row):
    peers = lax.axis_size("seq")
    groups = lax.axis_size("tp")
    member = lax.axis_index("tp")
    spans, neighbours = nbr_shard.shape
    requested = spans * neighbours
    tokens_here, width = query.shape
    heads_here = width // HD
    stored, quarter, features = encoded.shape
    capacity = max(2, 2 * requested // peers)
    owner_shard = nbr_shard.reshape(requested)
    store_row = nbr_row.reshape(requested)
    owners = jnp.arange(peers, dtype=jnp.int32)
    one_hot = (owner_shard[:, None] == owners[None, :]).astype(jnp.int32)
    earlier = jnp.cumsum(one_hot, axis=0) - one_hot
    slot_index = jnp.sum(earlier * one_hot, axis=1)
    request = jnp.full((peers, capacity), -1, jnp.int32).at[owner_shard, slot_index].set(store_row)
    asked = lax.all_to_all(request, "seq", split_axis=0, concat_axis=0, tiled=True)
    picked = jnp.take(encoded, jnp.maximum(asked, 0), axis=0)
    answer = lax.all_to_all(picked, "seq", split_axis=0, concat_axis=0, tiled=True)
    fetched = answer[owner_shard, slot_index]
    key_split = key_weight.reshape(features, groups, width)
    value_split = value_weight.reshape(features, groups, width)
    own_keys = lax.dynamic_index_in_dim(key_split, member, 1, keepdims=False)
    own_values = lax.dynamic_index_in_dim(value_split, member, 1, keepdims=False)
    own_joined = jnp.concatenate([own_keys, own_values], 1)
    key_value = jnp.einsum(
        "rte,ef->rtf",
        lax.all_gather(fetched, "tp", axis=1, tiled=True),
        own_joined,
        preferred_element_type=jnp.float32,
    ).astype(jnp.bfloat16)
    full_len = key_value.shape[1]
    key_rows = key_value[:, :, :width].reshape(spans, neighbours * full_len, heads_here, HD)
    value_rows = key_value[:, :, width:].reshape(spans, neighbours * full_len, heads_here, HD)
    shifted = shift_rows(query).reshape(spans, SPAN, heads_here, HD)
    grad_shift = shift_rows(d_attended).reshape(spans, SPAN, heads_here, HD)
    blended, grad_shifted, grad_keys, grad_values = attend(
        shifted, grad_shift, key_rows, value_rows
    )
    attended = unshift_rows(blended.reshape(tokens_here, width)).astype(jnp.bfloat16)
    d_query = unshift_rows(grad_shifted.reshape(tokens_here, width)).astype(jnp.bfloat16)
    grad_joined = jnp.concatenate(
        [
            grad_keys.reshape(requested, full_len, width),
            grad_values.reshape(requested, full_len, width),
        ],
        2,
    )
    partial_term = jnp.einsum(
        "rtf,ef->rte", grad_joined, own_joined, preferred_element_type=jnp.float32
    )
    d_nbr = lax.psum_scatter(partial_term, "tp", scatter_dimension=1, tiled=True).astype(
        jnp.bfloat16
    )
    parcel = (
        jnp.zeros((peers, capacity, quarter, features), jnp.bfloat16)
        .at[owner_shard, slot_index]
        .set(d_nbr)
    )
    arrived = lax.all_to_all(parcel, "seq", split_axis=0, concat_axis=0, tiled=True)
    target = jnp.where(asked >= 0, asked, stored).reshape(peers * capacity)
    summed = jax.ops.segment_sum(
        arrived.reshape(peers * capacity, quarter, features).astype(jnp.float32),
        target,
        num_segments=stored + 1,
    )
    d_encoded = summed[:stored].astype(jnp.bfloat16)
    return (attended, d_query, d_encoded)


def solution(mesh):
    placed = (
        P("seq", "tp"),
        P("seq", "tp"),
        P("seq", "tp", None),
        P(),
        P(),
        P("seq", None),
        P("seq", None),
    )
    return jax.shard_map(
        shards,
        mesh=mesh,
        in_specs=placed,
        out_specs=(P("seq", "tp"), P("seq", "tp"), P("seq", "tp", None)),
        check_vma=False,
    )
```

profile of v0, /device:TPU:16, one launch (start us, length us, event | category | flops | bytes accessed | tf_op | source)
XLA Modules:
  0.0 732.6 jit_solution(1935442412856443175)
XLA Ops:
  11.6 19.5 %all_to_all.22 = s32[64,1,2]{2,1,0:T(1,128)S(1)} all-to-all(s32[64,1,2]{2,1,0:T(1,128)S(1)} %copy.45), channel_id=1, replica_groups=mesh['seq'=64,'tp'=4] {'seq'}, dimensions={0} | all-to-all | bytes 1024 | tf_op jit(solution)/shard_map/all_to_all | solution.py:59
  41.6 170.0 %all_to_all.23 = bf16[64,2,32,896]{3,2,1,0:T(8,128)(2,1)} all-to-all(bf16[64,2,32,896]{3,2,1,0:T(8,128)(2,1)S(1)} %broadcast_select_fusion), channel_id=1, replica_groups=mesh['seq'=64,'tp'=4] {'seq'}, dimensions={0} | all-to-all | bytes 14680064 | tf_op jit(solution)/shard_map/all_to_all | solution.py:61
  218.4 7.2 reshape.137
  225.5 7.3 %reshape.138 = bf16[896,4,512]{2,1,0:T(4,128)(2,1)} reshape(bf16[896,2048]{1,0:T(8,128)(2,1)} %param.11) | data formatting | bytes 7340032 | tf_op jit(solution)/shard_map/reshape | solution.py:64
  232.9 6.9 constant_dynamic-slice_fusion
  240.3 38.5 %all-gather.2.cloned.1.call-done = bf16[26,128,896]{2,1,0:T(8,128)(2,1)} async-done(((bf16[26,32,896]{2,1,0:T(8,128)(2,1)}), bf16[26,128,896]{2,1,0:T(8,128)(2,1)}) %all-gather.2.cloned.1.call-update) | async-done | bytes 5963792 | tf_op jit(solution)/shard_map/all_gather | solution.py:70
  278.9 10.3 %convolution_convert_fusion = bf16[26,128,1024]{2,1,0:T(8,128)(2,1)S(1)} fusion(bf16[26,128,896]{2,1,0:T(8,128)(2,1)} %all-gather.2.cloned.1.call-done, bf16[896,512]{1,0:T(8,128)(2,1)S(1)} %bitcast.55, bf16[896,512]{1,0:T(8,128)(2,1)S(1)} %bitcast.57), kind=kOutput, calls=%fused_computation.9 | convolution fusion | flops 6113984512 | bytes 14614528 | tf_op jit(solution)/shard_map/rte,ef->rtf/dot_general | solution.py:68
  292.8 7.0 reshape.141
  299.8 7.2 reshape.139
  317.6 11.2 %convert_bitcast_fusion = bf16[13,256,4,128]{1,3,2,0:T(8,128)(2,1)} fusion(bf16[13,64,4,128]{3,2,1,0:T(4,128)(2,1)S(1)} %reshape.143, f32[13,4,64]{2,1,0:T(4,128)} %get-tuple-element.9, f32[13,4,64,256]{3,2,1,0:T(8,128)} %copy-done.2), kind=kOutput, calls=%fused_computation.14 | convolution fusion | flops 224071168 | bytes 7681024 | tf_op jit(solution)/shard_map/chqk,cqhd->ckhd/dot_general | solution.py:36
  328.8 25.0 %convert_bitcast_fusion.1 = bf16[13,256,4,128]{1,3,2,0:T(8,128)(2,1)} fusion(f32[13,4,64,256]{3,2,1,0:T(8,128)} %fusion.7, bf16[13,64,4,128]{3,2,1,0:T(4,128)(2,1)S(1)} %reshape.140, f32[13,4,64,256]{3,2,1,0:T(8,128)} %get-tuple-element.10, f32[13,4,64]{2,1,0:T(4,128)} %get-tuple-element.9), kind=kOutput, calls=%fused_computation.15 | convolution fusion | flops 225775104 | bytes 11088896 | tf_op jit(solution)/shard_map/chqk,cqhd->ckhd/dot_general | solution.py:33
  353.8 6.6 copy.59
  360.5 6.8 reshape.145
  367.3 6.6 copy.61
  373.9 6.8 reshape.146
  380.7 12.0 %fusion.2 = f32[26,128,896]{2,1,0:T(8,128)} fusion(bf16[26,128,512]{2,1,0:T(8,128)(2,1)} %reshape.146, bf16[26,128,512]{2,1,0:T(8,128)(2,1)} %reshape.145, bf16[896,512]{1,0:T(8,128)(2,1)S(1)} %bitcast.56, bf16[896,512]{1,0:T(8,128)(2,1)S(1)} %bitcast.58), kind=kOutput, calls=%fused_computation.10 | convolution fusion | flops 6124208128 | bytes 20578304 | tf_op jit(solution)/shard_map/rtf,ef->rte/dot_general | solution.py:91
  392.7 112.6 %reduce-scatter.2.cloned.1.call-done = f32[26,32,896]{2,1,0:T(8,128)} async-done(((f32[26,128,896]{2,1,0:T(8,128)}), f32[26,32,896]{2,1,0:T(8,128)}) %reduce-scatter.2.cloned.1.call-update) | async-done | bytes 2981904 | tf_op jit(solution)/shard_map/reduce_scatter | solution.py:94
  511.2 5.5 scatter_fusion.1
  516.7 11.1 %all-to-all-start.2 = ((bf16[64,2,32,896]{3,2,1,0:T(8,128)(2,1)}), bf16[64,2,32,896]{3,2,1,0:T(8,128)(2,1)}, u32[]{:S(2)}, u32[]{:S(2)}) async-start(bf16[64,2,32,896]{3,2,1,0:T(8,128)(2,1)} %scatter_fusion.1), calls=%async_computation.3 | async-start | bytes 14680064 | tf_op jit(solution)/shard_map/all_to_all | solution.py:102
  528.0 24.3 %fusion.35 = bf16[13,64,4,128]{3,1,2,0:T(8,128)(2,1)S(1)} fusion(bf16[13,256,4,128]{3,2,1,0:T(4,128)(2,1)} %reshape.141, f32[13,4,64,256]{3,2,1,0:T(8,128)} %fusion.7, f32[13,4,64,256]{3,2,1,0:T(8,128)} %get-tuple-element.10, f32[13,4,64]{2,1,0:T(4,128)S(1)} %copy-done.7), kind=kOutput, calls=%fused_computation.38 | convolution fusion | flops 224497152 | bytes 11088896 | tf_op jit(solution)/shard_map/chqk,ckhd->cqhd/dot_general | solution.py:32
  553.2 9.9 %fusion.40 = bf16[13,64,4,128]{3,1,2,0:T(8,128)(2,1)S(1)} fusion(bf16[13,256,4,128]{3,2,1,0:T(4,128)(2,1)} %reshape.139, f32[13,4,64]{2,1,0:T(4,128)S(1)} %copy-done.7, f32[13,4,64,256]{3,2,1,0:T(8,128)} %copy-done.2), kind=kOutput, calls=%fused_computation.39 | convolution fusion | flops 222793216 | bytes 7681024 | tf_op jit(solution)/shard_map/chqk,ckhd->cqhd/dot_general | solution.py:28
  566.2 125.2 %all-to-all-done.2 = bf16[64,2,32,896]{3,2,1,0:T(8,128)(2,1)} async-done(((bf16[64,2,32,896]{3,2,1,0:T(8,128)(2,1)}), bf16[64,2,32,896]{3,2,1,0:T(8,128)(2,1)}, u32[]{:S(2)}, u32[]{:S(2)}) %all-to-all-start.2) | async-done | bytes 7340064 | tf_op jit(solution)/shard_map/all_to_all | solution.py:102
  691.4 10.3 %bitcast_convert_fusion = f32[128,32,896]{2,1,0:T(8,128)} fusion(bf16[64,2,32,896]{3,2,1,0:T(8,128)(2,1)} %all-to-all-done.2), kind=kLoop, calls=%fused_computation.7 | loop fusion | flops 3670016 | bytes 22020096 | tf_op jit(solution)/shard_map/convert_element_type | solution.py:105
  701.9 22.4 %scatter_fusion.2 = f32[17,32,896]{2,1,0:T(8,128)S(1)} fusion(f32[17,32,896]{2,1,0:T(8,128)S(1)} %broadcast_in_dim.34, s32[128]{0:T(128)S(1)} %fusion.51, f32[128,32,896]{2,1,0:T(8,128)} %bitcast_convert_fusion), kind=kCustom, calls=%fused_computation.4 | custom fusion | flops 3670016 | bytes 44040704 | tf_op jit(solution)/shard_map/scatter-add | solution.py:104
  (68 shorter events, 47.6 us)
Async XLA Ops:
  7.2 26.2 %copy-start = (bf16[16,32,896]{2,1,0:T(8,128)(2,1)S(1)}, bf16[16,32,896]{2,1,0:T(8,128)(2,1)}, u32[]{:S(2)}) copy-start(bf16[16,32,896]{2,1,0:T(8,128)(2,1)} %param.9) | copy-start | bytes 2752516
  7.2 271.7 %all-gather.2.cloned.1.call-start = ((), (), s32[]{:S(2)}) async-start(), calls=%async_computation.4 | async-start | bytes 7454720 | tf_op jit(solution)/shard_map/all_gather | solution.py:70
  211.7 5.6 copy-start.4
  216.7 1.2 copy-start.5
  216.8 288.5 %reduce-scatter.2.cloned.1.call-start = ((), (), s32[]{:S(2)}) async-start(), calls=%async_computation.5 | async-start | bytes 14909440 | tf_op jit(solution)/shard_map/reduce_scatter | solution.py:94
  310.2 3.5 copy-start.2
  310.2 4.4 copy-start.3
  516.7 11.1 %copy-start.6 = (s32[64,2]{1,0:T(8,128)S(1)}, s32[64,2]{1,0:T(8,128)}, u32[]{:S(2)}) copy-start(s32[64,2]{1,0:T(8,128)} %get-tuple-element.3) | copy-start | bytes 1540
  516.7 11.3 %copy-start.7 = (f32[13,4,64]{2,1,0:T(4,128)S(1)}, f32[13,4,64]{2,1,0:T(4,128)}, u32[]{:S(2)}) copy-start(f32[13,4,64]{2,1,0:T(4,128)} %get-tuple-element.9) | copy-start | bytes 39940
  516.7 174.7 %all-to-all-start.2 = ((bf16[64,2,32,896]{3,2,1,0:T(8,128)(2,1)}), bf16[64,2,32,896]{3,2,1,0:T(8,128)(2,1)}, u32[]{:S(2)}, u32[]{:S(2)}) async-start(bf16[64,2,32,896]{3,2,1,0:T(8,128)(2,1)} %scatter_fusion.1), calls=%async_computation.3 | async-start | bytes 14680064 | tf_op jit(solution)/shard_map/all_to_all | solution.py:102
  701.9 23.4 %copy-start.1 = (bf16[16,32,896]{2,1,0:T(8,128)(2,1)S(1)}, bf16[16,32,896]{2,1,0:T(8,128)(2,1)}, u32[]{:S(2)}) copy-start(bf16[16,32,896]{2,1,0:T(8,128)(2,1)} %param.9) | copy-start | bytes 2752516
Sparse Core Ops, SparseCore 0:
  216.9 61.9 all-gather.1
  392.8 112.3 reduce-scatter.1
where the time goes:
time: 739 us; the launch traced here: 733 us
  waiting for transfers between devices  276 us (37%)
  blocking collectives  190 us (26%)
  matrix products  98.9 us (13%)
  local copies, waits for them, and re-layouts  97.9 us (13%)
  other arithmetic  43.5 us (6%)
  between operations  14.7 us (2%)
  starting transfers between devices  11.6 us (2%)
    all_to_all x1, blocking collectives, shards(): lax.all_to_all(picked, 'seq', split_axis=0, concat_axis=0, tiled=True)  170 us
    all_to_all x1, waiting for transfers between devices, shards(): lax.all_to_all(parcel, 'seq', split_axis=0, concat_axis=0, tiled=True)  125 us
    reduce_scatter x1, waiting for transfers between devices, shards(): lax.psum_scatter(partial_term, 'tp', scatter_dimension=1, tiled=True)  113 us
    all_gather x1, waiting for transfers between devices, shards(): lax.all_gather(fetched, 'tp', axis=1, tiled=True)  38.5 us
    dot_general x1, matrix products, attend(): jnp.einsum('chqk,cqhd->ckhd', grad_scores, shifted, preferred_element_typ...  25 us
    dot_general x1, matrix products, attend(): jnp.einsum('chqk,ckhd->cqhd', grad_scores, key_rows, preferred_element_ty...  24.3 us
    scatter-add x1, other arithmetic, shards(): jax.ops.segment_sum(arrived.reshape(peers * capacity, quarter, features)....  22.4 us
    all_to_all x1, blocking collectives, shards(): lax.all_to_all(request, 'seq', split_axis=0, concat_axis=0, tiled=True)  19.5 us
  transfers between devices with their start and end apart: 3, of which 3 were waited for; matrix products, arithmetic and copies ran while one was open for 8% of the time, Pallas kernels for 0%

commit v1 on v0

v1 whole, which is shorter than its diff:
```python
import jax
import jax.numpy as jnp
from jax import lax
from jax.experimental import pallas as pl
from jax.experimental.pallas import tpu as pltpu
from jax.sharding import Mesh, PartitionSpec as P

HD = 128
SPAN = 64
LANES = 8
PIECE = 4
WIDTHS = (256, 256, 384)
BF = jnp.bfloat16
F32 = jnp.float32
VMEM_BYTES = 48 * 1024 * 1024


def matmul(left, right, left_dim=1, right_dim=0):
    return lax.dot_general(
        left, right, (((left_dim,), (right_dim,)), ((), ())), preferred_element_type=F32
    )


def bounds(widths):
    starts = [0]
    for width in widths:
        starts.append(starts[-1] + width)
    return list(zip(starts[:-1], starts[1:]))


def reorder_matrix(size, stored, quarter):
    to = lax.broadcasted_iota(jnp.int32, (size, size), 0)
    source = lax.broadcasted_iota(jnp.int32, (size, size), 1)
    lane = to // (stored * PIECE)
    row = (to // PIECE) % stored
    token = to % PIECE
    return (source == row * quarter + lane * PIECE + token).astype(F32).astype(BF)


def split_pieces(encoded):
    stored, quarter, features = encoded.shape
    size = stored * quarter

    def kernel(enc_ref, *outs):
        order = reorder_matrix(size, stored, quarter)
        for out, (start, end) in zip(outs, bounds(WIDTHS)):
            out[...] = matmul(order, enc_ref[:, start:end]).astype(BF)

    return pl.pallas_call(
        kernel,
        out_shape=[jax.ShapeDtypeStruct((size, width), BF) for width in WIDTHS],
        compiler_params=pltpu.CompilerParams(vmem_limit_bytes=VMEM_BYTES),
        cost_estimate=pl.CostEstimate(
            flops=2 * size * size * features, bytes_accessed=4 * size * features, transcendentals=0
        ),
        name="split_pieces",
    )(encoded.reshape(size, features))


def join_pieces(parts, stored, quarter, features):
    size = stored * quarter

    def kernel(*refs):
        out_ref = refs[-1]
        order = reorder_matrix(size, stored, quarter)
        for part, (start, end) in zip(refs[:-1], bounds(WIDTHS)):
            out_ref[:, start:end] = matmul(order, part[...], 0, 0).astype(BF)

    joined = pl.pallas_call(
        kernel,
        out_shape=jax.ShapeDtypeStruct((size, features), BF),
        compiler_params=pltpu.CompilerParams(vmem_limit_bytes=VMEM_BYTES),
        cost_estimate=pl.CostEstimate(
            flops=2 * size * size * features, bytes_accessed=4 * size * features, transcendentals=0
        ),
        name="join_pieces",
    )(*parts)
    return joined.reshape(stored, quarter, features)


def pick_rows(store, target):
    planes, rows, width = store.shape
    picks = target.shape[0]

    def kernel(target_ref, store_ref, out_ref, total):
        step = pl.program_id(0)
        row = lax.broadcasted_iota(jnp.int32, (picks, rows), 1) + step * rows
        one_hot = (row == target_ref[...]).astype(F32).astype(BF)
        term = matmul(one_hot, store_ref[0])

        @pl.when(step == 0)
        def _():
            total[...] = term

        @pl.when(step > 0)
        def _():
            total[...] += term

        @pl.when(step == planes - 1)
        def _():
            out_ref[...] = total[...].astype(BF)

    return pl.pallas_call(
        kernel,
        grid=(planes,),
        in_specs=[
            pl.BlockSpec((picks, 1), lambda i: (0, 0)),
            pl.BlockSpec((1, rows, width), lambda i: (i, 0, 0)),
        ],
        out_specs=pl.BlockSpec((picks, width), lambda i: (0, 0)),
        out_shape=jax.ShapeDtypeStruct((picks, width), BF),
        scratch_shapes=[pltpu.VMEM((picks, width), F32)],
        compiler_params=pltpu.CompilerParams(vmem_limit_bytes=VMEM_BYTES),
        cost_estimate=pl.CostEstimate(
            flops=2 * picks * planes * rows * width,
            bytes_accessed=2 * (picks + planes * rows) * width,
            transcendentals=0,
        ),
        name="pick_rows",
    )(target, store)


def sum_rows(terms, target, planes, rows):
    picks, width = terms.shape

    def kernel(target_ref, terms_ref, out_ref):
        step = pl.program_id(0)
        row = lax.broadcasted_iota(jnp.int32, (rows, picks), 0) + step * rows
        one_hot = (row == target_ref[...]).astype(F32).astype(BF)
        out_ref[0] = matmul(one_hot, terms_ref[...]).astype(BF)

    return pl.pallas_call(
        kernel,
        grid=(planes,),
        in_specs=[
            pl.BlockSpec((1, picks), lambda i: (0, 0)),
            pl.BlockSpec((picks, width), lambda i: (0, 0)),
        ],
        out_specs=pl.BlockSpec((1, rows, width), lambda i: (i, 0, 0)),
        out_shape=jax.ShapeDtypeStruct((planes, rows, width), BF),
        compiler_params=pltpu.CompilerParams(vmem_limit_bytes=VMEM_BYTES),
        cost_estimate=pl.CostEstimate(
            flops=2 * picks * planes * rows * width,
            bytes_accessed=2 * (picks + planes * rows) * width,
            transcendentals=0,
        ),
        name="sum_rows",
    )(target, terms)


def attend_spans(member, fetched, key_weight, value_weight, query, d_attended):
    groups, spans, piece_rows, _ = fetched[0].shape
    keys = groups * piece_rows
    features = key_weight.shape[0]
    tokens, width = query.shape
    heads = width // HD
    factor = HD ** (-0.5)
    chunks = len(WIDTHS)

    def kernel(member_ref, *refs):
        parts = refs[:chunks]
        wk_ref, wv_ref, q0_ref, q1_ref, g0_ref, g1_ref = refs[chunks : chunks + 6]
        att_ref, dq_ref = refs[chunks + 6 : chunks + 8]
        outs = refs[chunks + 8 : 2 * chunks + 8]
        last_att, last_dq = refs[2 * chunks + 8 :]
        span = pl.program_id(0)

        @pl.when(span == 0)
        def _():
            last_att[...] = jnp.zeros_like(last_att)
            last_dq[...] = jnp.zeros_like(last_dq)

        rows = jnp.concatenate(
            [part[:, 0].astype(F32).reshape(keys, part.shape[3]).astype(BF) for part in parts], 1
        )
        wk = wk_ref[...]
        wv = wv_ref[...]
        key_rows = matmul(rows, wk).astype(BF)
        value_rows = matmul(rows, wv).astype(BF)

        to = lax.broadcasted_iota(jnp.int32, (SPAN, 2 * SPAN), 0)
        source = lax.broadcasted_iota(jnp.int32, (SPAN, 2 * SPAN), 1)
        inside = (source < SPAN) | (span < spans - 1)
        ahead = ((source == to + SPAN - 1) & inside).astype(F32).astype(BF)
        back = (source == to + 1).astype(F32).astype(BF)
        shifted = matmul(ahead, jnp.concatenate([q0_ref[...], q1_ref[...]], 0)).astype(BF)
        grad_shift = matmul(ahead, jnp.concatenate([g0_ref[...], g1_ref[...]], 0)).astype(BF)

        blended, grad_shifted, grad_keys, grad_values = [], [], [], []
        for head in range(heads):
            cols = slice(head * HD, (head + 1) * HD)
            q, g, k, v = shifted[:, cols], grad_shift[:, cols], key_rows[:, cols], value_rows[:, cols]
            scores = matmul(q, k, 1, 1) * factor
            weights = jnp.exp(scores - jnp.max(scores, axis=1, keepdims=True))
            probs = weights / jnp.sum(weights, axis=1, keepdims=True)
            probs_b = probs.astype(BF)
            blended.append(matmul(probs_b, v))
            grad_probs = matmul(g, v, 1, 1)
            inner = jnp.sum(probs * grad_probs, axis=1, keepdims=True)
            grad_scores = (probs * (grad_probs - inner) * factor).astype(BF)
            grad_shifted.append(matmul(grad_scores, k))
            grad_keys.append(matmul(grad_scores, q, 0, 0))
            grad_values.append(matmul(probs_b, g, 0, 0))
        now_att = jnp.concatenate(blended, 1).astype(BF)
        now_dq = jnp.concatenate(grad_shifted, 1).astype(BF)
        att_ref[...] = matmul(back, jnp.concatenate([last_att[...], now_att], 0)).astype(BF)
        dq_ref[...] = matmul(back, jnp.concatenate([last_dq[...], now_dq], 0)).astype(BF)
        last_att[...] = now_att
        last_dq[...] = now_dq
        gk = jnp.concatenate(grad_keys, 1).astype(BF)
        gv = jnp.concatenate(grad_values, 1).astype(BF)
        for out, (start, end) in zip(outs, bounds(WIDTHS)):
            term = matmul(gk, wk[start:end], 1, 1) + matmul(gv, wv[start:end], 1, 1)
            out[...] = term.reshape(groups, 1, piece_rows, end - start).astype(BF)

    def this(i, m):
        return (i, 0)

    def following(i, m):
        return (jnp.minimum(i + 1, spans - 1), 0)

    block = (SPAN, width)
    part_specs = [
        pl.BlockSpec((groups, 1, piece_rows, w), lambda i, m: (0, i, 0, 0)) for w in WIDTHS
    ]
    weight_spec = pl.BlockSpec((features, width), lambda i, m: (0, m[0]))
    return pl.pallas_call(
        kernel,
        grid_spec=pltpu.PrefetchScalarGridSpec(
            num_scalar_prefetch=1,
            grid=(spans,),
            in_specs=part_specs
            + [
                weight_spec,
                weight_spec,
                pl.BlockSpec(block, this),
                pl.BlockSpec(block, following),
                pl.BlockSpec(block, this),
                pl.BlockSpec(block, following),
            ],
            out_specs=[pl.BlockSpec(block, this), pl.BlockSpec(block, this)] + part_specs,
            scratch_shapes=[pltpu.VMEM(block, BF), pltpu.VMEM(block, BF)],
        ),
        out_shape=[jax.ShapeDtypeStruct((tokens, width), BF)] * 2
        + [jax.ShapeDtypeStruct((groups, spans, piece_rows, w), BF) for w in WIDTHS],
        compiler_params=pltpu.CompilerParams(vmem_limit_bytes=VMEM_BYTES),
        cost_estimate=pl.CostEstimate(
            flops=spans * (8 * keys * features * width + 14 * SPAN * keys * width),
            bytes_accessed=4 * spans * keys * features + 8 * tokens * width,
            transcendentals=spans * heads * SPAN * keys,
        ),
        name="attend_spans",
    )(member, *fetched, key_weight, value_weight, query, query, d_attended, d_attended)


def shards(query, d_attended, encoded, key_weight, value_weight, nbr_shard, nbr_row):
    plane = ("y", "c")
    planes = lax.axis_size("z")
    groups = lax.axis_size("x")
    member = lax.axis_index("x").astype(jnp.int32).reshape(1)
    spans, neighbours = nbr_shard.shape
    stored, quarter, features = encoded.shape
    rows = LANES * stored * PIECE
    requested = spans * neighbours * PIECE

    picks = (nbr_shard * stored + nbr_row).reshape(spans * neighbours)
    all_picks = lax.all_gather(picks, plane, tiled=True)
    target = (all_picks[:, None] * PIECE + jnp.arange(PIECE, dtype=jnp.int32)[None, :]).reshape(-1)

    fetched = []
    for piece in split_pieces(encoded):
        piece = lax.all_to_all(piece, plane, 0, 0, tiled=True)
        store = lax.all_gather(piece, "z", axis=0, tiled=False)
        picked = pick_rows(store, target.reshape(-1, 1))
        mine = lax.all_to_all(picked, plane, 0, 0, tiled=True)
        every = lax.all_gather(mine, "x", axis=0, tiled=False)
        fetched.append(every.reshape(groups * LANES, spans, neighbours * PIECE, -1))

    attended, d_query, *terms = attend_spans(
        member, fetched, key_weight, value_weight, query, d_attended
    )

    returned = []
    for term in terms:
        width = term.shape[-1]
        swapped = lax.all_to_all(
            term.reshape(groups, LANES * requested, width), "x", 0, 0, tiled=True
        )
        d_nbr = jnp.sum(swapped.astype(F32), axis=0).astype(BF)
        home = lax.all_to_all(d_nbr, plane, 0, 0, tiled=True)
        sums = sum_rows(home, target.reshape(1, -1), planes, rows)
        reduced = lax.psum_scatter(sums, "z", scatter_dimension=0, tiled=True)
        reduced = reduced.reshape(rows, width)
        returned.append(lax.all_to_all(reduced, plane, 0, 0, tiled=True))
    d_encoded = join_pieces(returned, stored, quarter, features)
    return (attended, d_query, d_encoded)


def solution(mesh):
    groups = mesh.devices.shape[1]
    fine = Mesh(mesh.devices.reshape(-1, LANES // 2, 2, groups), ("z", "y", "c", "x"))
    seq = ("z", "y", "c")
    placed = (
        P(seq, "x"),
        P(seq, "x"),
        P(seq, "x", None),
        P(),
        P(),
        P(seq, None),
        P(seq, None),
    )
    return jax.shard_map(
        shards,
        mesh=fine,
        in_specs=placed,
        out_specs=(P(seq, "x"), P(seq, "x"), P(seq, "x", None)),
        check_vma=False,
    )
```

time: 739 us -> 511 us (0.69)
  matrix products: 98.9 us -> 0 us
  waiting for transfers between devices: 276 us -> 178 us
  local copies, waits for them, and re-layouts: 97.9 us -> 7.54 us
  Pallas kernels: 0 us -> 82.4 us
  other arithmetic: 43.5 us -> 2.51 us
  blocking collectives: 190 us -> 210 us
    all_to_all x1 -> x2, waiting for transfers between devices: 125 us -> 10.4 us  [the longest x1 6.02 us: shards(): home = lax.all_to_all(d_nbr, plane, 0, 0, tiled=True)]
    all_gather x1 -> x6, waiting for transfers between devices: 38.5 us -> 143 us  [the longest x3 79.2 us: shards(): every = lax.all_gather(mine, 'x', axis=0, tiled=False)]
    dot_general x8 -> x0, matrix products: 98.9 us -> none  [the longest x1 25 us: attend(): jnp.einsum('chqk,cqhd->ckhd', grad_scores, shifted, preferred_element_typ...]
    reduce_scatter x1 -> x3, waiting for transfers between devices: 113 us -> 25.3 us  [shards(): reduced = lax.psum_scatter(sums, 'z', scatter_dimension=0, tiled=True)]
    pallas_call x0 -> x9, Pallas kernels: none -> 82.4 us  [the longest x1 48.9 us: attend_spans(): pl.pallas_call(kernel, grid_spec=pltpu.PrefetchScalarGridSpec(num_scalar_...]
    reshape x10 -> x1, local copies, waits for them, and re-layouts: 42.8 us -> 0.08 us  [shards(): picks = (nbr_shard * stored + nbr_row).reshape(spans * neighbours)]
    scatter-add x1 -> x0, other arithmetic: 22.4 us -> none  [shards(): jax.ops.segment_sum(arrived.reshape(peers * capacity, quarter, features)....]
    convert_element_type x2 -> x0, local copies, waits for them, and re-layouts: 13.3 us -> none  [the longest x1 6.65 us: attend(): grad_keys = jnp.einsum('chqk,cqhd->ckhd', grad_scores, shifted, preferred...]
  transfers between devices with their start and end apart: 3 -> 11, of which waited for: 3 -> 9; matrix products, arithmetic and copies ran while one was open for 8% -> 1% of each run, Pallas kernels for 0% -> 5%
where the time goes in v1:
time: 511 us; the launch traced here: 507 us
  blocking collectives  210 us (41%)
  waiting for transfers between devices  178 us (35%)
  Pallas kernels  82.4 us (16%)
  between operations  14.6 us (3%)
  starting transfers between devices  11.1 us (2%)
  local copies, waits for them, and re-layouts  7.54 us (1%)
    all_to_all x3, blocking collectives, shards(): lax.all_to_all(term.reshape(groups, LANES * requested, width), 'x', 0, 0,...  85.1 us
    all_gather x3, waiting for transfers between devices, shards(): every = lax.all_gather(mine, 'x', axis=0, tiled=False)  79.2 us
    all_gather x3, waiting for transfers between devices, shards(): store = lax.all_gather(piece, 'z', axis=0, tiled=False)  63.5 us
    pallas_call x1, Pallas kernels, attend_spans(): pl.pallas_call(kernel, grid_spec=pltpu.PrefetchScalarGridSpec(num_scalar_...  48.9 us
    all_to_all x3, blocking collectives, shards(): mine = lax.all_to_all(picked, plane, 0, 0, tiled=True)  36.1 us
    all_to_all x3, blocking collectives, shards(): piece = lax.all_to_all(piece, plane, 0, 0, tiled=True)  32.6 us
    all_to_all x2, blocking collectives, shards(): home = lax.all_to_all(d_nbr, plane, 0, 0, tiled=True)  25.7 us
    reduce_scatter x3, waiting for transfers between devices, shards(): reduced = lax.psum_scatter(sums, 'z', scatter_dimension=0, tiled=True)  25.3 us
  transfers between devices with their start and end apart: 11, of which 9 were waited for; matrix products, arithmetic and copies ran while one was open for 1% of the time, Pallas kernels for 5%

profile of v1, /device:TPU:16, one launch (start us, length us, event | category | flops | bytes accessed | tf_op | source)
XLA Modules:
  0.0 506.6 jit_solution(17750390677216425542)
XLA Ops:
  9.1 9.5 %all_to_all.135 = bf16[8,64,256]{2,1,0:T(8,128)(2,1)} all-to-all(bf16[8,64,256]{2,1,0:T(8,128)(2,1)S(1)} %bitcast.47), channel_id=1, replica_groups=mesh['z'=8,'y'=4,'c'=2,'x'=4] {'y','c'}, dimensions={0} | all-to-all | bytes 524288 | tf_op jit(solution)/shard_map/all_to_all | solution.py:272
  18.7 10.6 %all_to_all.136 = bf16[8,64,256]{2,1,0:T(8,128)(2,1)} all-to-all(bf16[8,64,256]{2,1,0:T(8,128)(2,1)S(1)} %bitcast.46), channel_id=1, replica_groups=mesh['z'=8,'y'=4,'c'=2,'x'=4] {'y','c'}, dimensions={0} | all-to-all | bytes 524288 | tf_op jit(solution)/shard_map/all_to_all | solution.py:272
  29.4 12.5 %all_to_all.137 = bf16[8,64,384]{2,1,0:T(8,128)(2,1)} all-to-all(bf16[8,64,384]{2,1,0:T(8,128)(2,1)S(1)} %bitcast.45), channel_id=1, replica_groups=mesh['z'=8,'y'=4,'c'=2,'x'=4] {'y','c'}, dimensions={0} | all-to-all | bytes 786432 | tf_op jit(solution)/shard_map/all_to_all | solution.py:272
  43.7 8.6 %all-reduce = s32[208]{0:T(256)S(1)} all-reduce(s32[208]{0:T(256)S(1)} %dynamic-update-slice), channel_id=1, replica_groups=mesh['z'=8,'y'=4,'c'=2,'x'=4] {'y','c'}, use_global_device_ids=true, to_apply=%add | all-reduce | flops 208 | bytes 1664
  52.5 10.6 %all-gather.11.cloned.1.call-done.store_ref = bf16[8,512,256]{2,1,0:T(8,128)(2,1)} async-done(((bf16[1,512,256]{2,1,0:T(8,128)(2,1)}), bf16[8,512,256]{2,1,0:T(8,128)(2,1)}) %all-gather.11.cloned.1.call-update) | async-done | bytes 2097168 | tf_op jit(solution)/shard_map/all_gather | solution.py:273
  68.9 11.2 %all_to_all.138 = bf16[8,104,256]{2,1,0:T(8,128)(2,1)} all-to-all(bf16[8,104,256]{2,1,0:T(8,128)(2,1)S(1)} %bitcast.42), channel_id=1, replica_groups=mesh['z'=8,'y'=4,'c'=2,'x'=4] {'y','c'}, dimensions={0} | all-to-all | bytes 851968 | tf_op jit(solution)/shard_map/all_to_all | solution.py:275
  80.2 24.6 %all-gather.7.cloned.1.call-done.store_ref = bf16[8,512,256]{2,1,0:T(8,128)(2,1)} async-done(((bf16[1,512,256]{2,1,0:T(8,128)(2,1)}), bf16[8,512,256]{2,1,0:T(8,128)(2,1)}) %all-gather.7.cloned.1.call-update) | async-done | bytes 2097168 | tf_op jit(solution)/shard_map/all_gather | solution.py:273
  110.5 11.2 %all_to_all.139 = bf16[8,104,256]{2,1,0:T(8,128)(2,1)} all-to-all(bf16[8,104,256]{2,1,0:T(8,128)(2,1)S(1)} %bitcast.43), channel_id=1, replica_groups=mesh['z'=8,'y'=4,'c'=2,'x'=4] {'y','c'}, dimensions={0} | all-to-all | bytes 851968 | tf_op jit(solution)/shard_map/all_to_all | solution.py:275
  121.8 28.3 %all-gather.15.cloned.1.call-done.store_ref = bf16[8,512,384]{2,1,0:T(8,128)(2,1)} async-done(((bf16[1,512,384]{2,1,0:T(8,128)(2,1)}), bf16[8,512,384]{2,1,0:T(8,128)(2,1)}) %all-gather.15.cloned.1.call-update) | async-done | bytes 3145744 | tf_op jit(solution)/shard_map/all_gather | solution.py:273
  152.0 6.3 %pick_rows.5 = bf16[832,384]{1,0:T(8,128)(2,1)S(1)} custom-call(s32[832,1]{1,0:T(8,128)S(1)} %add.50.target_ref, bf16[8,512,384]{2,1,0:T(8,128)(2,1)S(1)} %copy-done), custom_call_target="tpu_custom_call" | custom-call | flops 2617245696 | bytes 3784704 | tf_op jit(solution)/shard_map/pick_rows/pallas_call | solution.py:103
  158.3 13.7 %all_to_all.140 = bf16[8,104,384]{2,1,0:T(8,128)(2,1)} all-to-all(bf16[8,104,384]{2,1,0:T(8,128)(2,1)S(1)} %bitcast.39), channel_id=1, replica_groups=mesh['z'=8,'y'=4,'c'=2,'x'=4] {'y','c'}, dimensions={0} | all-to-all | bytes 1277952 | tf_op jit(solution)/shard_map/all_to_all | solution.py:275
  172.0 8.5 %all-gather.13.cloned.1.call-done = bf16[4,832,256]{2,1,0:T(8,128)(2,1)} async-done(((bf16[1,832,256]{2,1,0:T(8,128)(2,1)}), bf16[4,832,256]{2,1,0:T(8,128)(2,1)}) %all-gather.13.cloned.1.call-update) | async-done | bytes 1703952 | tf_op jit(solution)/shard_map/all_gather | solution.py:276
  180.5 31.8 %all-gather.9.cloned.1.call-done = bf16[4,832,256]{2,1,0:T(8,128)(2,1)} async-done(((bf16[1,832,256]{2,1,0:T(8,128)(2,1)}), bf16[4,832,256]{2,1,0:T(8,128)(2,1)}) %all-gather.9.cloned.1.call-update) | async-done | bytes 1703952 | tf_op jit(solution)/shard_map/all_gather | solution.py:276
  212.3 38.8 %all-gather.17.cloned.1.call-done = bf16[4,832,384]{2,1,0:T(8,128)(2,1)} async-done(((bf16[1,832,384]{2,1,0:T(8,128)(2,1)}), bf16[4,832,384]{2,1,0:T(8,128)(2,1)}) %all-gather.17.cloned.1.call-update) | async-done | bytes 2555920 | tf_op jit(solution)/shard_map/all_gather | solution.py:276
  251.2 48.9 %attend_spans.1 = (bf16[832,512]{1,0:T(8,128)(2,1)}, bf16[832,512]{1,0:T(8,128)(2,1)}, bf16[32,13,8,256]{3,2,1,0:T(8,128)(2,1)S(1)}, bf16[32,13,8,256]{3,2,1,0:T(8,128)(2,1)S(1)}, bf16[32,13,8,384]{3,2,1,0:T(8,128)(2,1)}) custom-call(s32[1]{0:T(128)} %bitcast.member_ref, bf16[32,13,8,256]{3,2,1,0:T(8,128)(2,1)} %bitcast.65, ...), custom_call_target="tpu_custom_call" | custom-call | flops 13740539904 | bytes 15335424 | tf_op jit(solution)/shard_map/attend_spans/pallas_call | solution.py:227
  300.1 25.0 %all_to_all.141 = bf16[4,832,256]{2,1,0:T(8,128)(2,1)S(1)} all-to-all(bf16[4,832,256]{2,1,0:T(8,128)(2,1)S(1)} %bitcast.35), channel_id=1, replica_groups=mesh['z'=8,'y'=4,'c'=2,'x'=4] {'x'}, dimensions={0} | all-to-all | bytes 3407872 | tf_op jit(solution)/shard_map/all_to_all | solution.py:286
  342.3 24.9 %all_to_all.142 = bf16[4,832,256]{2,1,0:T(8,128)(2,1)S(1)} all-to-all(bf16[4,832,256]{2,1,0:T(8,128)(2,1)S(1)} %bitcast.34), channel_id=1, replica_groups=mesh['z'=8,'y'=4,'c'=2,'x'=4] {'x'}, dimensions={0} | all-to-all | bytes 3407872 | tf_op jit(solution)/shard_map/all_to_all | solution.py:286
  367.7 11.8 %all_to_all.143 = bf16[8,104,256]{2,1,0:T(8,128)(2,1)S(1)} all-to-all(bf16[8,104,256]{2,1,0:T(8,128)(2,1)S(1)} %bitcast.55), channel_id=1, replica_groups=mesh['z'=8,'y'=4,'c'=2,'x'=4] {'y','c'}, dimensions={0} | all-to-all | bytes 851968 | tf_op jit(solution)/shard_map/all_to_all | solution.py:290
  384.6 35.1 %all_to_all.144 = bf16[4,832,384]{2,1,0:T(8,128)(2,1)S(1)} all-to-all(bf16[4,832,384]{2,1,0:T(8,128)(2,1)} %bitcast.49), channel_id=1, replica_groups=mesh['z'=8,'y'=4,'c'=2,'x'=4] {'x'}, dimensions={0} | all-to-all | bytes 5111808 | tf_op jit(solution)/shard_map/all_to_all | solution.py:286
  420.5 13.9 %all_to_all.145 = bf16[8,104,384]{2,1,0:T(8,128)(2,1)S(1)} all-to-all(bf16[8,104,384]{2,1,0:T(8,128)(2,1)S(1)} %bitcast.51), channel_id=1, replica_groups=mesh['z'=8,'y'=4,'c'=2,'x'=4] {'y','c'}, dimensions={0} | all-to-all | bytes 1277952 | tf_op jit(solution)/shard_map/all_to_all | solution.py:290
  434.4 6.3 %sum_rows.5 = bf16[8,512,384]{2,1,0:T(8,128)(2,1)} custom-call(s32[1,832]{1,0:T(1,128)S(1)} %add.47.target_ref, bf16[832,384]{1,0:T(8,128)(2,1)S(1)} %bitcast.40), custom_call_target="tpu_custom_call" | custom-call | flops 2617245696 | bytes 3784704 | tf_op jit(solution)/shard_map/sum_rows/pallas_call | solution.py:132
  451.2 10.9 %all_to_all.146 = bf16[8,64,256]{2,1,0:T(8,128)(2,1)S(1)} all-to-all(bf16[8,64,256]{2,1,0:T(8,128)(2,1)} %bitcast.62), channel_id=1, replica_groups=mesh['z'=8,'y'=4,'c'=2,'x'=4] {'y','c'}, dimensions={0} | all-to-all | bytes 524288 | tf_op jit(solution)/shard_map/all_to_all | solution.py:294
  462.1 25.2 %reduce-scatter.8.cloned.1.call-done = bf16[1,512,384]{2,1,0:T(8,128)(2,1)} async-done(((bf16[8,512,384]{2,1,0:T(8,128)(2,1)}), bf16[1,512,384]{2,1,0:T(8,128)(2,1)}) %reduce-scatter.8.cloned.1.call-update) | async-done | bytes 393232 | tf_op jit(solution)/shard_map/reduce_scatter | solution.py:292
  487.3 11.0 %all_to_all.147 = bf16[8,64,384]{2,1,0:T(8,128)(2,1)S(1)} all-to-all(bf16[8,64,384]{2,1,0:T(8,128)(2,1)} %bitcast.60), channel_id=1, replica_groups=mesh['z'=8,'y'=4,'c'=2,'x'=4] {'y','c'}, dimensions={0} | all-to-all | bytes 786432 | tf_op jit(solution)/shard_map/all_to_all | solution.py:294
  (61 shorter events, 52.6 us)
Async XLA Ops:
  7.2 55.9 %all-gather.11.cloned.1.call-start = ((), (), s32[]{:S(2)}) async-start(), calls=%async_computation.20 | async-start | bytes 2359296 | tf_op jit(solution)/shard_map/all_gather | solution.py:273
  7.2 1.2 copy-start.3
  8.4 33.6 %copy-start.6 = (s32[13,2]{0,1:T(2,128)S(1)}, s32[13,2]{0,1:T(2,128)}, u32[]{:S(2)}) copy-start(s32[13,2]{0,1:T(2,128)} %param.13) | copy-start | bytes 316
  8.4 33.6 %copy-start.7 = (s32[13,2]{0,1:T(2,128)S(1)}, s32[13,2]{0,1:T(2,128)}, u32[]{:S(2)}) copy-start(s32[13,2]{0,1:T(2,128)} %param.12) | copy-start | bytes 316
  8.4 33.8 %copy-start.8 = (u32[256]{0:T(256)S(1)}, u32[256]{0:T(256)}, u32[]{:S(2)}) copy-start(u32[256]{0:T(256)} %constant.18) | copy-start | bytes 3076
  18.6 86.1 %all-gather.7.cloned.1.call-start = ((), (), s32[]{:S(2)}) async-start(), calls=%async_computation.18 | async-start | bytes 2359296 | tf_op jit(solution)/shard_map/all_gather | solution.py:273
  29.3 120.8 %all-gather.15.cloned.1.call-start = ((), (), s32[]{:S(2)}) async-start(), calls=%async_computation.22 | async-start | bytes 3538944 | tf_op jit(solution)/shard_map/all_gather | solution.py:273
  41.9 138.7 %all-gather.13.cloned.1.call-start = ((), (), s32[]{:S(2)}) async-start(), calls=%async_computation.21 | async-start | bytes 2129920 | tf_op jit(solution)/shard_map/all_gather | solution.py:276
  63.1 1.6 copy-start.2
  80.1 132.2 %all-gather.9.cloned.1.call-start = ((), (), s32[]{:S(2)}) async-start(), calls=%async_computation.19 | async-start | bytes 2129920 | tf_op jit(solution)/shard_map/all_gather | solution.py:276
  104.7 1.6 copy-start.1
  121.7 129.4 %all-gather.17.cloned.1.call-start = ((), (), s32[]{:S(2)}) async-start(), calls=%async_computation.23 | async-start | bytes 3194880 | tf_op jit(solution)/shard_map/all_gather | solution.py:276
  150.1 1.9 copy-start
  152.0 99.2 %copy-start.4 = (bf16[832,512]{1,0:T(8,128)(2,1)S(1)}, bf16[832,512]{1,0:T(8,128)(2,1)}, u32[]{:S(2)}) copy-start(bf16[832,512]{1,0:T(8,128)(2,1)} %refs_6_.1) | copy-start | bytes 2555908
  152.0 99.2 %copy-start.5 = (bf16[832,512]{1,0:T(8,128)(2,1)S(1)}, bf16[832,512]{1,0:T(8,128)(2,1)}, u32[]{:S(2)}) copy-start(bf16[832,512]{1,0:T(8,128)(2,1)} %refs_8_.1) | copy-start | bytes 2555908
  326.2 10.9 %all-to-all-start.10 = ((bf16[8,104,256]{2,1,0:T(8,128)(2,1)}), bf16[8,104,256]{2,1,0:T(8,128)(2,1)S(1)}, u32[]{:S(2)}, u32[]{:S(2)}) async-start(bf16[8,104,256]{2,1,0:T(8,128)(2,1)} %bitcast.54), calls=%async_computation.11 | async-start | bytes 851968 | tf_op jit(solution)/shard_map/all_to_all | solution.py:290
  331.0 109.8 %reduce-scatter.6.cloned.1.call-start = ((), (), s32[]{:S(2)}) async-start(), calls=%async_computation.25 | async-start | bytes 2359296 | tf_op jit(solution)/shard_map/reduce_scatter | solution.py:292
  342.2 104.6 %reduce-scatter.4.cloned.1.call-start = ((), (), s32[]{:S(2)}) async-start(), calls=%async_computation.24 | async-start | bytes 2359296 | tf_op jit(solution)/shard_map/reduce_scatter | solution.py:292
  384.5 102.8 %reduce-scatter.8.cloned.1.call-start = ((), (), s32[]{:S(2)}) async-start(), calls=%async_computation.26 | async-start | bytes 3538944 | tf_op jit(solution)/shard_map/reduce_scatter | solution.py:292
  440.8 10.4 %all-to-all-start.11 = ((bf16[8,64,256]{2,1,0:T(8,128)(2,1)}), bf16[8,64,256]{2,1,0:T(8,128)(2,1)S(1)}, u32[]{:S(2)}, u32[]{:S(2)}) async-start(bf16[8,64,256]{2,1,0:T(8,128)(2,1)} %bitcast.61), calls=%async_computation.13 | async-start | bytes 524288 | tf_op jit(solution)/shard_map/all_to_all | solution.py:294
Sparse Core Ops, SparseCore 0:
  18.8 44.2 all-gather.10
  64.9 39.8 all-gather.6
  106.5 43.5 all-gather.14
  151.8 28.7 all-gather.12
  182.2 30.1 all-gather.8
  214.0 37.1 all-gather.16
  342.3 42.3 reduce-scatter.5
  387.3 40.6 reduce-scatter.3
  440.9 46.3 reduce-scatter.7

commit v2 on v1

v2 whole, which is shorter than its diff:
```python
import jax
import jax.numpy as jnp
from jax import lax
from jax.experimental import pallas as pl
from jax.experimental.pallas import tpu as pltpu
from jax.sharding import Mesh, PartitionSpec as P

HD = 128
SPAN = 64
LANES = 8
PIECE = 4
WIDTHS = (512, 384)
BF = jnp.bfloat16
F32 = jnp.float32
I32 = jnp.int32
PARAMS = pltpu.CompilerParams(vmem_limit_bytes=48 * 1024 * 1024)


def matmul(left, right, left_dim=1, right_dim=0):
    return lax.dot_general(
        left, right, (((left_dim,), (right_dim,)), ((), ())), preferred_element_type=F32
    )


def bounds(widths):
    starts = [0]
    for width in widths:
        starts.append(starts[-1] + width)
    return list(zip(starts[:-1], starts[1:]))


def cost(flops, bytes_accessed, transcendentals=0):
    return pl.CostEstimate(
        flops=int(flops), bytes_accessed=int(bytes_accessed), transcendentals=int(transcendentals)
    )


def send_ring(array, axis, step):
    size = lax.axis_size(axis)
    if step % size == 0:
        return array
    return lax.ppermute(array, axis, [(i, (i + step) % size) for i in range(size)])


def piece_matrix(plane_ref, away, stored, quarter):
    plane = (plane_ref[0] + away) % LANES
    shape = (stored * PIECE, stored * quarter)
    to = lax.broadcasted_iota(I32, shape, 0)
    source = lax.broadcasted_iota(I32, shape, 1)
    token = (to // PIECE) * quarter + to % PIECE + plane * PIECE
    return (source == token).astype(F32).astype(BF)


def split_pieces(encoded, plane):
    stored, quarter, features = encoded.shape
    size = stored * quarter

    def kernel(plane_ref, enc_ref, *outs):
        order = jnp.concatenate(
            [piece_matrix(plane_ref, away, stored, quarter) for away in range(LANES)], 0
        )
        step = stored * PIECE
        for chunk, (start, end) in enumerate(bounds(WIDTHS)):
            pieces = matmul(order, enc_ref[:, start:end]).astype(BF)
            for away in range(LANES):
                outs[chunk * LANES + away][...] = pieces[away * step : (away + 1) * step]

    outs = pl.pallas_call(
        kernel,
        in_specs=[pl.BlockSpec(memory_space=pltpu.SMEM), pl.BlockSpec(memory_space=pltpu.VMEM)],
        out_shape=[
            jax.ShapeDtypeStruct((stored * PIECE, width), BF)
            for width in WIDTHS
            for _ in range(LANES)
        ],
        compiler_params=PARAMS,
        cost_estimate=cost(2 * size * size * features, 4 * size * features),
        name="split_pieces",
    )(plane, encoded.reshape(size, features))
    return [outs[i * LANES : (i + 1) * LANES] for i in range(len(WIDTHS))]


def join_pieces(parts, plane, stored, quarter, features):
    size = stored * quarter

    def kernel(plane_ref, *refs):
        out_ref = refs[-1]
        order = jnp.concatenate(
            [piece_matrix(plane_ref, away, stored, quarter) for away in range(LANES)], 0
        )
        for chunk, (start, end) in enumerate(bounds(WIDTHS)):
            pieces = [ref[...] for ref in refs[chunk * LANES : (chunk + 1) * LANES]]
            out_ref[:, start:end] = matmul(order, jnp.concatenate(pieces, 0), 0, 0).astype(BF)

    joined = pl.pallas_call(
        kernel,
        in_specs=[pl.BlockSpec(memory_space=pltpu.SMEM)]
        + [pl.BlockSpec(memory_space=pltpu.VMEM)] * (LANES * len(WIDTHS)),
        out_shape=jax.ShapeDtypeStruct((size, features), BF),
        compiler_params=PARAMS,
        cost_estimate=cost(2 * size * size * features, 4 * size * features),
        name="join_pieces",
    )(plane, *[piece for part in parts for piece in part])
    return joined.reshape(stored, quarter, features)


def pick_rows(stores, target, other=None):
    rows, width = stores[0].shape
    blocks = len(stores)
    picks = target.shape[0]
    parts = 1 if other is None else LANES
    each = picks // parts
    extra = [] if other is None else [other]

    def kernel(target_ref, *refs):
        total = None if other is None else refs[blocks][...].astype(F32)
        outs = refs[blocks + len(extra) :]
        column = lax.broadcasted_iota(I32, (picks, rows), 1)
        for block in range(blocks):
            one_hot = (column == target_ref[...] - block * rows).astype(F32).astype(BF)
            term = matmul(one_hot, refs[block][...])
            total = term if total is None else total + term
        for part in range(parts):
            outs[part][...] = total[part * each : (part + 1) * each].astype(BF)

    return pl.pallas_call(
        kernel,
        out_shape=[jax.ShapeDtypeStruct((each, width), BF)] * parts,
        compiler_params=PARAMS,
        cost_estimate=cost(
            2 * picks * blocks * rows * width, 2 * (picks + blocks * rows) * width
        ),
        name="pick_rows",
    )(target, *stores, *extra)


def sum_rows(terms, target, blocks, rows):
    width = terms[0].shape[1]
    picks = target.shape[1]
    count = len(terms)

    def kernel(target_ref, *refs):
        joined = jnp.concatenate([ref[...] for ref in refs[:count]], 0)
        row = lax.broadcasted_iota(I32, (rows, picks), 0)
        for block in range(blocks):
            one_hot = (row == target_ref[...] - block * rows).astype(F32).astype(BF)
            refs[count + block][...] = matmul(one_hot, joined).astype(BF)

    return pl.pallas_call(
        kernel,
        out_shape=[jax.ShapeDtypeStruct((rows, width), BF)] * blocks,
        compiler_params=PARAMS,
        cost_estimate=cost(
            2 * picks * blocks * rows * width, 2 * (picks + blocks * rows) * width
        ),
        name="sum_rows",
    )(target, *terms)


def add_and_cut(terms, parts):
    rows, width = terms[0].shape
    each = rows // parts
    count = len(terms)

    def kernel(*refs):
        total = refs[0][...].astype(F32)
        for ref in refs[1:count]:
            total = total + ref[...].astype(F32)
        for part in range(parts):
            refs[count + part][...] = total[part * each : (part + 1) * each].astype(BF)

    return pl.pallas_call(
        kernel,
        out_shape=[jax.ShapeDtypeStruct((each, width), BF)] * parts,
        compiler_params=PARAMS,
        cost_estimate=cost(count * rows * width, 2 * (count + 1) * rows * width),
        name="add_and_cut",
    )(*terms)


def attend_spans(member, fetched, key_weight, value_weight, query, d_attended):
    groups = len(fetched[0])
    spans, piece_rows = fetched[0][0].shape[1:3]
    here = LANES * piece_rows
    keys = groups * here
    features = key_weight.shape[0]
    tokens, width = query.shape
    heads = width // HD
    factor = HD ** (-0.5)
    count = len(WIDTHS) * groups

    def kernel(member_ref, *refs):
        parts = refs[:count]
        wk_ref, wv_ref, q0_ref, q1_ref, g0_ref, g1_ref = refs[count : count + 6]
        att_ref, dq_ref = refs[count + 6 : count + 8]
        outs = refs[count + 8 : 2 * count + 8]
        last_att, last_dq = refs[2 * count + 8 :]
        span = pl.program_id(0)

        @pl.when(span == 0)
        def _():
            last_att[...] = jnp.zeros_like(last_att)
            last_dq[...] = jnp.zeros_like(last_dq)

        def chunk_rows(chunk):
            pieces = [
                part[:, 0].astype(F32).reshape(here, part.shape[3])
                for part in parts[chunk * groups : (chunk + 1) * groups]
            ]
            return jnp.concatenate(pieces, 0).astype(BF)

        rows = jnp.concatenate([chunk_rows(chunk) for chunk in range(len(WIDTHS))], 1)
        wk = wk_ref[...]
        wv = wv_ref[...]
        key_rows = matmul(rows, wk).astype(BF)
        value_rows = matmul(rows, wv).astype(BF)

        to = lax.broadcasted_iota(I32, (SPAN, 2 * SPAN), 0)
        source = lax.broadcasted_iota(I32, (SPAN, 2 * SPAN), 1)
        inside = (source < SPAN) | (span < spans - 1)
        ahead = ((source == to + SPAN - 1) & inside).astype(F32).astype(BF)
        back = (source == to + 1).astype(F32).astype(BF)
        shifted = matmul(ahead, jnp.concatenate([q0_ref[...], q1_ref[...]], 0)).astype(BF)
        grad_shift = matmul(ahead, jnp.concatenate([g0_ref[...], g1_ref[...]], 0)).astype(BF)

        cols = [slice(head * HD, (head + 1) * HD) for head in range(heads)]
        scores = [matmul(shifted[:, c], key_rows[:, c], 1, 1) * factor for c in cols]
        grad_probs = [matmul(grad_shift[:, c], value_rows[:, c], 1, 1) for c in cols]
        probs_b, grad_scores = [], []
        for score, grad in zip(scores, grad_probs):
            weights = jnp.exp(score - jnp.max(score, axis=1, keepdims=True))
            probs = weights / jnp.sum(weights, axis=1, keepdims=True)
            inner = jnp.sum(probs * grad, axis=1, keepdims=True)
            probs_b.append(probs.astype(BF))
            grad_scores.append((probs * (grad - inner) * factor).astype(BF))
        blended = [matmul(p, value_rows[:, c]) for p, c in zip(probs_b, cols)]
        grad_shifted = [matmul(s, key_rows[:, c]) for s, c in zip(grad_scores, cols)]
        grad_keys = [matmul(s, shifted[:, c], 0, 0) for s, c in zip(grad_scores, cols)]
        grad_values = [matmul(p, grad_shift[:, c], 0, 0) for p, c in zip(probs_b, cols)]
        now_att = jnp.concatenate(blended, 1).astype(BF)
        now_dq = jnp.concatenate(grad_shifted, 1).astype(BF)
        att_ref[...] = matmul(back, jnp.concatenate([last_att[...], now_att], 0)).astype(BF)
        dq_ref[...] = matmul(back, jnp.concatenate([last_dq[...], now_dq], 0)).astype(BF)
        last_att[...] = now_att
        last_dq[...] = now_dq
        gk = jnp.concatenate(grad_keys, 1).astype(BF)
        gv = jnp.concatenate(grad_values, 1).astype(BF)
        for chunk, (start, end) in enumerate(bounds(WIDTHS)):
            term = matmul(gk, wk[start:end], 1, 1) + matmul(gv, wv[start:end], 1, 1)
            for group in range(groups):
                piece = term[group * here : (group + 1) * here]
                outs[chunk * groups + group][...] = piece.reshape(
                    LANES, 1, piece_rows, end - start
                ).astype(BF)

    def this(i, m):
        return (i, 0)

    def following(i, m):
        return (jnp.minimum(i + 1, spans - 1), 0)

    block = (SPAN, width)
    part_specs = [
        pl.BlockSpec((LANES, 1, piece_rows, w), lambda i, m: (0, i, 0, 0))
        for w in WIDTHS
        for _ in range(groups)
    ]
    weight_spec = pl.BlockSpec((features, width), lambda i, m: (0, m[0]))
    outs = pl.pallas_call(
        kernel,
        grid_spec=pltpu.PrefetchScalarGridSpec(
            num_scalar_prefetch=1,
            grid=(spans,),
            in_specs=part_specs
            + [
                weight_spec,
                weight_spec,
                pl.BlockSpec(block, this),
                pl.BlockSpec(block, following),
                pl.BlockSpec(block, this),
                pl.BlockSpec(block, following),
            ],
            out_specs=[pl.BlockSpec(block, this), pl.BlockSpec(block, this)] + part_specs,
            scratch_shapes=[pltpu.VMEM(block, BF), pltpu.VMEM(block, BF)],
        ),
        out_shape=[jax.ShapeDtypeStruct((tokens, width), BF)] * 2
        + [
            jax.ShapeDtypeStruct((LANES, spans, piece_rows, w), BF)
            for w in WIDTHS
            for _ in range(groups)
        ],
        compiler_params=PARAMS,
        cost_estimate=cost(
            spans * (8 * keys * features * width + 14 * SPAN * keys * width),
            4 * spans * keys * features + 8 * tokens * width,
            spans * heads * SPAN * keys,
        ),
        name="attend_spans",
    )(
        member,
        *[part for parts in fetched for part in parts],
        key_weight,
        value_weight,
        query,
        query,
        d_attended,
        d_attended,
    )
    terms = [outs[2 + i * groups : 2 + (i + 1) * groups] for i in range(len(WIDTHS))]
    return outs[0], outs[1], terms


def shards(query, d_attended, encoded, key_weight, value_weight, nbr_shard, nbr_row):
    planes = lax.axis_size("z")
    groups = lax.axis_size("x")
    columns = lax.axis_size("y")
    z, y, c, x = [lax.axis_index(axis).astype(I32) for axis in ("z", "y", "c", "x")]
    spans, neighbours = nbr_shard.shape
    stored, quarter, features = encoded.shape
    rows = planes * stored * PIECE
    plane = z.reshape(1)

    own = []
    for pieces in split_pieces(encoded, plane):
        own.append(
            jnp.concatenate([send_ring(piece, "z", k) for k, piece in enumerate(pieces)], 0)
        )

    picks = (nbr_shard * stored + nbr_row).reshape(spans * neighbours)
    picks, own[0] = lax.optimization_barrier((picks, own[0]))
    picks = lax.all_gather(picks, ("z", "c"), tiled=True).reshape(planes, 2, -1)
    picks = jnp.roll(jnp.roll(picks, -z, 0), -c, 1).transpose(1, 0, 2)
    store = picks // stored
    away_y = (y - store // 2 % columns) % columns
    away_z = (z - store // (2 * columns)) % planes
    first = away_y * rows + away_z * (stored * PIECE) + picks % stored * PIECE
    first = jnp.where(store % 2 == c, first, -columns * rows)
    target = (first[..., None] + jnp.arange(PIECE, dtype=I32)).reshape(2, -1)

    fetched = []
    for chunk, width in enumerate(WIDTHS):
        gathered = [send_ring(own[chunk], "y", a) for a in range(columns)]
        (theirs,) = pick_rows(gathered, target[1].reshape(-1, 1))
        picked = pick_rows(gathered, target[0].reshape(-1, 1), send_ring(theirs, "c", 1))
        mine = jnp.concatenate([send_ring(part, "z", r) for r, part in enumerate(picked)], 0)
        fetched.append(
            [
                send_ring(mine, "x", away).reshape(LANES, spans, neighbours * PIECE, width)
                for away in range(groups)
            ]
        )

    attended, d_query, terms = attend_spans(
        x.reshape(1), fetched, key_weight, value_weight, query, d_attended
    )

    returned = []
    for chunk, parts in enumerate(terms):
        width = WIDTHS[chunk]
        arrived = [
            send_ring(part.reshape(-1, width), "x", -away) for away, part in enumerate(parts)
        ]
        d_nbr = add_and_cut(arrived, planes)
        home = jnp.concatenate([send_ring(part, "z", -r) for r, part in enumerate(d_nbr)], 0)
        sums = sum_rows([home, send_ring(home, "c", 1)], target.reshape(1, -1), columns, rows)
        whole = add_and_cut([send_ring(part, "y", -a) for a, part in enumerate(sums)], planes)
        returned.append([send_ring(part, "z", -k) for k, part in enumerate(whole)])
    d_encoded = join_pieces(returned, plane, stored, quarter, features)
    return (attended, d_query, d_encoded)


def solution(mesh):
    groups = mesh.devices.shape[1]
    fine = Mesh(mesh.devices.reshape(-1, LANES // 2, 2, groups), ("z", "y", "c", "x"))
    seq = ("z", "y", "c")
    placed = (
        P(seq, "x"),
        P(seq, "x"),
        P(seq, "x", None),
        P(),
        P(),
        P(seq, None),
        P(seq, None),
    )
    return jax.shard_map(
        shards,
        mesh=fine,
        in_specs=placed,
        out_specs=(P(seq, "x"), P(seq, "x"), P(seq, "x", None)),
        check_vma=False,
    )
```

time: 511 us -> 443 us (0.87)
  blocking collectives: 210 us -> 12.9 us
  starting transfers between devices: 11.1 us -> 167 us
  Pallas kernels: 82.4 us -> 54.3 us
  between operations: 14.6 us -> 2.22 us
  waiting for transfers between devices: 178 us -> 184 us
    all_to_all x13 -> x0, blocking collectives: 201 us -> none  [the longest x3 85.1 us: shards(): lax.all_to_all(term.reshape(groups, LANES * requested, width), 'x', 0, 0,...]
    ppermute x0 -> x84, waiting for transfers between devices: none -> 184 us  [send_ring(): lax.ppermute(array, axis, [(i, (i + step) % size) for i in range(size)])]
    ppermute x0 -> x84, starting transfers between devices: none -> 167 us  [send_ring(): lax.ppermute(array, axis, [(i, (i + step) % size) for i in range(size)])]
    all_gather x6 -> x0, waiting for transfers between devices: 143 us -> none  [the longest x3 79.2 us: shards(): every = lax.all_gather(mine, 'x', axis=0, tiled=False)]
    reduce_scatter x3 -> x0, waiting for transfers between devices: 25.3 us -> none  [shards(): reduced = lax.psum_scatter(sums, 'z', scatter_dimension=0, tiled=True)]
    pallas_call x1, Pallas kernels: 48.9 us -> 32.2 us  [attend_spans(): pl.pallas_call(kernel, grid_spec=pltpu.PrefetchScalarGridSpec(num_scalar_...]
    pallas_call x8 -> x12, Pallas kernels: 33.5 us -> 22.1 us  [the longest x4 10.7 us: pick_rows(): pl.pallas_call(kernel, out_shape=[jax.ShapeDtypeStruct((each, width), BF)...]
    all_to_all x2 -> x0, starting transfers between devices: 10.8 us -> none  [the longest x1 6.01 us: shards(): returned.append(lax.all_to_all(reduced, plane, 0, 0, tiled=True))]
  transfers between devices with their start and end apart: 11 -> 84, of which waited for: 9 -> 35; matrix products, arithmetic and copies ran while one was open for 1% -> 2% of each run, Pallas kernels for 5% -> 5%
where the time goes in v2:
time: 443 us; the launch traced here: 434 us
  waiting for transfers between devices  184 us (42%)
  starting transfers between devices  167 us (38%)
  Pallas kernels  54.3 us (12%)
  blocking collectives  12.9 us (3%)
  local copies, waits for them, and re-layouts  12.2 us (3%)
    ppermute x84, waiting for transfers between devices, send_ring(): lax.ppermute(array, axis, [(i, (i + step) % size) for i in range(size)])  184 us
    ppermute x84, starting transfers between devices, send_ring(): lax.ppermute(array, axis, [(i, (i + step) % size) for i in range(size)])  167 us
    pallas_call x1, Pallas kernels, attend_spans(): pl.pallas_call(kernel, grid_spec=pltpu.PrefetchScalarGridSpec(num_scalar_...  32.2 us
    unnamed x1, blocking collectives  12.9 us
    unnamed x65, local copies, waits for them, and re-layouts  10.7 us
    pallas_call x4, Pallas kernels, pick_rows(): pl.pallas_call(kernel, out_shape=[jax.ShapeDtypeStruct((each, width), BF)...  10.7 us
  transfers between devices with their start and end apart: 84, of which 35 were waited for; matrix products, arithmetic and copies ran while one was open for 2% of the time, Pallas kernels for 5%

profile of v2, /device:TPU:16, one launch (start us, length us, event | category | flops | bytes accessed | tf_op | source)
XLA Modules:
  0.0 434.1 jit_solution(8248450583453854971)
XLA Ops:
  7.8 4.0 collective-permute-start.23
  12.4 4.9 %collective-permute-start.25 = (bf16[64,384]{1,0:T(8,128)(2,1)S(1)}, bf16[64,384]{1,0:T(8,128)(2,1)S(1)}, u32[]{:S(2)}, u32[]{:S(2)}) collective-permute-start(bf16[64,384]{1,0:T(8,128)(2,1)S(1)} %get-tuple-element.110), channel_id=1, source_target_pairs={{0,160},{32,192},{64,224},{96,0},{128,32},{160,64},{192,96},{224,1... | collective-permute-start | bytes 147464 | tf_op jit(solution)/shard_map/ppermute | solution.py:42
  27.3 4.1 collective-permute-start.3
  46.5 12.9 %all-reduce = s32[416]{0:T(512)S(1)} all-reduce(s32[416]{0:T(512)S(1)} %dynamic-update-slice), channel_id=1, replica_groups=mesh['z'=8,'y'=4,'c'=2,'x'=4] {'z','c'}, use_global_device_ids=true, to_apply=%add | all-reduce | flops 416 | bytes 3328
  71.9 6.2 %collective-permute-done.7.refs_1_ = bf16[512,512]{1,0:T(8,128)(2,1)} collective-permute-done((bf16[512,512]{1,0:T(8,128)(2,1)S(1)}, bf16[512,512]{1,0:T(8,128)(2,1)}, u32[]{:S(2)}, u32[]{:S(2)}) %collective-permute-start.7) | collective-permute-done | bytes 524320 | tf_op jit(solution)/shard_map/ppermute | solution.py:42
  90.1 4.8 %collective-permute-start.35 = (bf16[104,384]{1,0:T(8,128)(2,1)S(1)}, bf16[104,384]{1,0:T(8,128)(2,1)S(1)}, u32[]{:S(2)}, u32[]{:S(2)}) collective-permute-start(bf16[104,384]{1,0:T(8,128)(2,1)S(1)} %get-tuple-element.117), channel_id=1, source_target_pairs={{0,128},{32,160},{64,192},{96,224},{128,0},{160,32},{192,64},{224,... | collective-permute-start | bytes 239624 | tf_op jit(solution)/shard_map/ppermute | solution.py:42
  98.4 4.8 %collective-permute-start.38 = (bf16[104,384]{1,0:T(8,128)(2,1)S(1)}, bf16[104,384]{1,0:T(8,128)(2,1)S(1)}, u32[]{:S(2)}, u32[]{:S(2)}) collective-permute-start(bf16[104,384]{1,0:T(8,128)(2,1)S(1)} %get-tuple-element.120), channel_id=1, source_target_pairs={{0,224},{32,0},{64,32},{96,64},{128,96},{160,128},{192,160},{224,1... | collective-permute-start | bytes 239624 | tf_op jit(solution)/shard_map/ppermute | solution.py:42
  123.5 4.2 collective-permute-start.15
  128.3 4.4 %collective-permute-done.12 = bf16[104,512]{1,0:T(8,128)(2,1)S(1)} collective-permute-done((bf16[104,512]{1,0:T(8,128)(2,1)S(1)}, bf16[104,512]{1,0:T(8,128)(2,1)S(1)}, u32[]{:S(2)}, u32[]{:S(2)}) %collective-permute-start.12) | collective-permute-done | bytes 106528 | tf_op jit(solution)/shard_map/ppermute | solution.py:42
  145.0 4.0 collective-permute-start.40
  149.1 50.0 %collective-permute-done.40 = bf16[832,384]{1,0:T(8,128)(2,1)S(1)} collective-permute-done((bf16[832,384]{1,0:T(8,128)(2,1)S(1)}, bf16[832,384]{1,0:T(8,128)(2,1)S(1)}, u32[]{:S(2)}, u32[]{:S(2)}) %collective-permute-start.40) | collective-permute-done | bytes 639008 | tf_op jit(solution)/shard_map/ppermute | solution.py:42
  199.2 12.3 %collective-permute-done.39 = bf16[832,384]{1,0:T(8,128)(2,1)S(1)} collective-permute-done((bf16[832,384]{1,0:T(8,128)(2,1)S(1)}, bf16[832,384]{1,0:T(8,128)(2,1)S(1)}, u32[]{:S(2)}, u32[]{:S(2)}) %collective-permute-start.39) | collective-permute-done | bytes 639008 | tf_op jit(solution)/shard_map/ppermute | solution.py:42
  211.5 32.2 %attend_spans.1 = (bf16[832,512]{1,0:T(8,128)(2,1)}, bf16[832,512]{1,0:T(8,128)(2,1)}, bf16[8,13,8,512]{3,2,1,0:T(8,128)(2,1)S(1)}, bf16[8,13,8,512]{3,2,1,0:T(8...) custom-call(s32[1]{0:T(128)} %bitcast.member_ref, ...), custom_call_target="tpu_custom_call" | custom-call | flops 13740539904 | bytes 15335424 | tf_op jit(solution)/shard_map/attend_spans/pallas_call | solution.py:269
  250.0 11.0 %collective-permute-done.63.refs_1_ = bf16[832,384]{1,0:T(8,128)(2,1)S(1)} collective-permute-done((bf16[832,384]{1,0:T(8,128)(2,1)S(1)}, bf16[832,384]{1,0:T(8,128)(2,1)S(1)}, u32[]{:S(2)}, u32[]{:S(2)}) %collective-permute-start.63) | collective-permute-done | bytes 639008 | tf_op jit(solution)/shard_map/ppermute | solution.py:42
  261.1 12.0 %collective-permute-start.44 = (bf16[832,512]{1,0:T(8,128)(2,1)}, bf16[832,512]{1,0:T(8,128)(2,1)S(1)}, u32[]{:S(2)}, u32[]{:S(2)}) collective-permute-start(bf16[832,512]{1,0:T(8,128)(2,1)} %bitcast.36), channel_id=1, source_target_pairs={{0,1},{1,2},{2,3},{3,0},{4,5},{5,6},{6,7},{7,4},{8,9},{9,10},{10,1... | collective-permute-start | bytes 2555912 | tf_op jit(solution)/shard_map/ppermute | solution.py:42
  273.1 4.0 collective-permute-done.65.refs_3_
  281.3 4.2 collective-permute-done.66
  285.6 4.7 %collective-permute-done.67 = bf16[104,384]{1,0:T(8,128)(2,1)S(1)} collective-permute-done((bf16[104,384]{1,0:T(8,128)(2,1)S(1)}, bf16[104,384]{1,0:T(8,128)(2,1)S(1)}, u32[]{:S(2)}, u32[]{:S(2)}) %collective-permute-start.67) | collective-permute-done | bytes 79904 | tf_op jit(solution)/shard_map/ppermute | solution.py:42
  290.2 5.6 %collective-permute-done.68 = bf16[104,384]{1,0:T(8,128)(2,1)S(1)} collective-permute-done((bf16[104,384]{1,0:T(8,128)(2,1)S(1)}, bf16[104,384]{1,0:T(8,128)(2,1)S(1)}, u32[]{:S(2)}, u32[]{:S(2)}) %collective-permute-start.68) | collective-permute-done | bytes 79904 | tf_op jit(solution)/shard_map/ppermute | solution.py:42
  295.9 4.6 %collective-permute-start.70 = (bf16[104,384]{1,0:T(8,128)(2,1)S(1)}, bf16[104,384]{1,0:T(8,128)(2,1)S(1)}, u32[]{:S(2)}, u32[]{:S(2)}) collective-permute-start(bf16[104,384]{1,0:T(8,128)(2,1)S(1)} %get-tuple-element.156), channel_id=1, source_target_pairs={{0,96},{32,128},{64,160},{96,192},{128,224},{160,0},{192,32},{224,... | collective-permute-start | bytes 239624 | tf_op jit(solution)/shard_map/ppermute | solution.py:42
  326.3 4.1 collective-permute-start.50
  330.5 4.0 collective-permute-done.47
  358.9 29.0 %collective-permute-done.75.refs_2_ = bf16[512,384]{1,0:T(8,128)(2,1)S(1)} collective-permute-done((bf16[512,384]{1,0:T(8,128)(2,1)S(1)}, bf16[512,384]{1,0:T(8,128)(2,1)S(1)}, u32[]{:S(2)}, u32[]{:S(2)}) %collective-permute-start.75) | collective-permute-done | bytes 393248 | tf_op jit(solution)/shard_map/ppermute | solution.py:42
  388.0 7.3 %collective-permute-done.76.refs_3_ = bf16[512,384]{1,0:T(8,128)(2,1)S(1)} collective-permute-done((bf16[512,384]{1,0:T(8,128)(2,1)S(1)}, bf16[512,384]{1,0:T(8,128)(2,1)S(1)}, u32[]{:S(2)}, u32[]{:S(2)}) %collective-permute-start.76) | collective-permute-done | bytes 393248 | tf_op jit(solution)/shard_map/ppermute | solution.py:42
  (241 shorter events, 192.3 us)
Async XLA Ops:
  37.4 23.3 %collective-permute-start.30 = (bf16[512,384]{1,0:T(8,128)(2,1)S(1)}, bf16[512,384]{1,0:T(8,128)(2,1)S(1)}, u32[]{:S(2)}, u32[]{:S(2)}) collective-permute-start(bf16[512,384]{1,0:T(8,128)(2,1)S(1)} %constant_dynamic-update-slice_fusion.16.refs_0_), channel_id=1, source_target_pairs={{0,24},{8,0},{16,8},{24,16},{1,25},{9,1},{17,9},{25,17},{2,26},{10... | collective-permute-start | bytes 1179656 | tf_op jit(solution)/shard_map/ppermute | solution.py:42
  38.0 22.9 %collective-permute-start.29 = (bf16[512,384]{1,0:T(8,128)(2,1)S(1)}, bf16[512,384]{1,0:T(8,128)(2,1)S(1)}, u32[]{:S(2)}, u32[]{:S(2)}) collective-permute-start(bf16[512,384]{1,0:T(8,128)(2,1)S(1)} %constant_dynamic-update-slice_fusion.16.refs_0_), channel_id=1, source_target_pairs={{0,16},{8,24},{16,0},{24,8},{1,17},{9,25},{17,1},{25,9},{2,18},{10... | collective-permute-start | bytes 1179656 | tf_op jit(solution)/shard_map/ppermute | solution.py:42
  41.4 19.4 %collective-permute-start.28 = (bf16[512,384]{1,0:T(8,128)(2,1)S(1)}, bf16[512,384]{1,0:T(8,128)(2,1)S(1)}, u32[]{:S(2)}, u32[]{:S(2)}) collective-permute-start(bf16[512,384]{1,0:T(8,128)(2,1)S(1)} %constant_dynamic-update-slice_fusion.16.refs_0_), channel_id=1, source_target_pairs={{0,8},{8,16},{16,24},{24,0},{1,9},{9,17},{17,25},{25,1},{2,10},{10... | collective-permute-start | bytes 1179656 | tf_op jit(solution)/shard_map/ppermute | solution.py:42
  43.0 26.4 %collective-permute-start.9 = (bf16[512,512]{1,0:T(8,128)(2,1)S(1)}, bf16[512,512]{1,0:T(8,128)(2,1)}, u32[]{:S(2)}, u32[]{:S(2)}) collective-permute-start(bf16[512,512]{1,0:T(8,128)(2,1)S(1)} %constant_dynamic-update-slice_fusion.refs_0_), channel_id=1, source_target_pairs={{0,24},{8,0},{16,8},{24,16},{1,25},{9,1},{17,9},{25,17},{2,26},{10... | collective-permute-start | bytes 1572872 | tf_op jit(solution)/shard_map/ppermute | solution.py:42
  43.7 28.2 %collective-permute-start.8 = (bf16[512,512]{1,0:T(8,128)(2,1)S(1)}, bf16[512,512]{1,0:T(8,128)(2,1)}, u32[]{:S(2)}, u32[]{:S(2)}) collective-permute-start(bf16[512,512]{1,0:T(8,128)(2,1)S(1)} %constant_dynamic-update-slice_fusion.refs_0_), channel_id=1, source_target_pairs={{0,16},{8,24},{16,0},{24,8},{1,17},{9,25},{17,1},{25,9},{2,18},{10... | collective-permute-start | bytes 1572872 | tf_op jit(solution)/shard_map/ppermute | solution.py:42
  81.4 30.7 %collective-permute-start.10 = (bf16[832,512]{1,0:T(8,128)(2,1)S(1)}, bf16[832,512]{1,0:T(8,128)(2,1)S(1)}, u32[]{:S(2)}, u32[]{:S(2)}) collective-permute-start(bf16[832,512]{1,0:T(8,128)(2,1)S(1)} %pick_rows.4), channel_id=1, source_target_pairs={{0,4},{4,0},{1,5},{5,1},{2,6},{6,2},{3,7},{7,3},{8,12},{12,8},{9,1... | collective-permute-start | bytes 2555912 | tf_op jit(solution)/shard_map/ppermute | solution.py:42
  109.2 39.7 %collective-permute-start.41 = (bf16[832,384]{1,0:T(8,128)(2,1)S(1)}, bf16[832,384]{1,0:T(8,128)(2,1)S(1)}, u32[]{:S(2)}, u32[]{:S(2)}) collective-permute-start(bf16[832,384]{1,0:T(8,128)(2,1)S(1)} %constant_dynamic-update-slice_fusion.24), channel_id=1, source_target_pairs={{0,3},{1,0},{2,1},{3,2},{4,7},{5,4},{6,5},{7,6},{8,11},{9,8},{10,9... | collective-permute-start | bytes 1916936 | tf_op jit(solution)/shard_map/ppermute | solution.py:42
  142.8 68.8 %collective-permute-start.20 = (bf16[832,512]{1,0:T(8,128)(2,1)}, bf16[832,512]{1,0:T(8,128)(2,1)}, u32[]{:S(2)}, u32[]{:S(2)}) collective-permute-start(bf16[832,512]{1,0:T(8,128)(2,1)} %constant_dynamic-update-slice_fusion.8), channel_id=1, source_target_pairs={{0,3},{1,0},{2,1},{3,2},{4,7},{5,4},{6,5},{7,6},{8,11},{9,8},{10,9... | collective-permute-start | bytes 2555912 | tf_op jit(solution)/shard_map/ppermute | solution.py:42
  143.6 68.0 %collective-permute-start.19 = (bf16[832,512]{1,0:T(8,128)(2,1)}, bf16[832,512]{1,0:T(8,128)(2,1)}, u32[]{:S(2)}, u32[]{:S(2)}) collective-permute-start(bf16[832,512]{1,0:T(8,128)(2,1)} %constant_dynamic-update-slice_fusion.8), channel_id=1, source_target_pairs={{0,2},{1,3},{2,0},{3,1},{4,6},{5,7},{6,4},{7,5},{8,10},{9,11},{10,... | collective-permute-start | bytes 2555912 | tf_op jit(solution)/shard_map/ppermute | solution.py:42
  144.1 67.4 %collective-permute-start.18 = (bf16[832,512]{1,0:T(8,128)(2,1)}, bf16[832,512]{1,0:T(8,128)(2,1)}, u32[]{:S(2)}, u32[]{:S(2)}) collective-permute-start(bf16[832,512]{1,0:T(8,128)(2,1)} %constant_dynamic-update-slice_fusion.8), channel_id=1, source_target_pairs={{0,1},{1,2},{2,3},{3,0},{4,5},{5,6},{6,7},{7,4},{8,9},{9,10},{10,1... | collective-permute-start | bytes 2555912 | tf_op jit(solution)/shard_map/ppermute | solution.py:42
  145.0 54.2 %collective-permute-start.40 = (bf16[832,384]{1,0:T(8,128)(2,1)S(1)}, bf16[832,384]{1,0:T(8,128)(2,1)S(1)}, u32[]{:S(2)}, u32[]{:S(2)}) collective-permute-start(bf16[832,384]{1,0:T(8,128)(2,1)S(1)} %constant_dynamic-update-slice_fusion.24), channel_id=1, source_target_pairs={{0,2},{1,3},{2,0},{3,1},{4,6},{5,7},{6,4},{7,5},{8,10},{9,11},{10,... | collective-permute-start | bytes 1916936 | tf_op jit(solution)/shard_map/ppermute | solution.py:42
  148.9 62.6 %collective-permute-start.39 = (bf16[832,384]{1,0:T(8,128)(2,1)S(1)}, bf16[832,384]{1,0:T(8,128)(2,1)S(1)}, u32[]{:S(2)}, u32[]{:S(2)}) collective-permute-start(bf16[832,384]{1,0:T(8,128)(2,1)S(1)} %constant_dynamic-update-slice_fusion.24), channel_id=1, source_target_pairs={{0,1},{1,2},{2,3},{3,0},{4,5},{5,6},{6,7},{7,4},{8,9},{9,10},{10,1... | collective-permute-start | bytes 1916936 | tf_op jit(solution)/shard_map/ppermute | solution.py:42
  244.5 28.6 %collective-permute-start.64 = (bf16[832,384]{1,0:T(8,128)(2,1)S(1)}, bf16[832,384]{1,0:T(8,128)(2,1)S(1)}, u32[]{:S(2)}, u32[]{:S(2)}) collective-permute-start(bf16[832,384]{1,0:T(8,128)(2,1)S(1)} %bitcast.31), channel_id=1, source_target_pairs={{0,2},{1,3},{2,0},{3,1},{4,6},{5,7},{6,4},{7,5},{8,10},{9,11},{10,... | collective-permute-start | bytes 1916936 | tf_op jit(solution)/shard_map/ppermute | solution.py:42
  245.0 32.1 %collective-permute-start.65 = (bf16[832,384]{1,0:T(8,128)(2,1)S(1)}, bf16[832,384]{1,0:T(8,128)(2,1)S(1)}, u32[]{:S(2)}, u32[]{:S(2)}) collective-permute-start(bf16[832,384]{1,0:T(8,128)(2,1)S(1)} %bitcast.30), channel_id=1, source_target_pairs={{0,1},{1,2},{2,3},{3,0},{4,5},{5,6},{6,7},{7,4},{8,9},{9,10},{10,1... | collective-permute-start | bytes 1916936 | tf_op jit(solution)/shard_map/ppermute | solution.py:42
  245.9 65.1 %collective-permute-start.42 = (bf16[832,512]{1,0:T(8,128)(2,1)}, bf16[832,512]{1,0:T(8,128)(2,1)S(1)}, u32[]{:S(2)}, u32[]{:S(2)}) collective-permute-start(bf16[832,512]{1,0:T(8,128)(2,1)} %bitcast.38), channel_id=1, source_target_pairs={{0,3},{1,0},{2,1},{3,2},{4,7},{5,4},{6,5},{7,6},{8,11},{9,8},{10,9... | collective-permute-start | bytes 2555912 | tf_op jit(solution)/shard_map/ppermute | solution.py:42
  248.5 62.5 %collective-permute-start.43 = (bf16[832,512]{1,0:T(8,128)(2,1)}, bf16[832,512]{1,0:T(8,128)(2,1)S(1)}, u32[]{:S(2)}, u32[]{:S(2)}) collective-permute-start(bf16[832,512]{1,0:T(8,128)(2,1)} %bitcast.37), channel_id=1, source_target_pairs={{0,2},{1,3},{2,0},{3,1},{4,6},{5,7},{6,4},{7,5},{8,10},{9,11},{10,... | collective-permute-start | bytes 2555912 | tf_op jit(solution)/shard_map/ppermute | solution.py:42
  261.1 50.9 %collective-permute-start.44 = (bf16[832,512]{1,0:T(8,128)(2,1)}, bf16[832,512]{1,0:T(8,128)(2,1)S(1)}, u32[]{:S(2)}, u32[]{:S(2)}) collective-permute-start(bf16[832,512]{1,0:T(8,128)(2,1)} %bitcast.36), channel_id=1, source_target_pairs={{0,1},{1,2},{2,3},{3,0},{4,5},{5,6},{6,7},{7,4},{8,9},{9,10},{10,1... | collective-permute-start | bytes 2555912 | tf_op jit(solution)/shard_map/ppermute | solution.py:42
  310.5 31.4 %collective-permute-start.73 = (bf16[832,384]{1,0:T(8,128)(2,1)S(1)}, bf16[832,384]{1,0:T(8,128)(2,1)S(1)}, u32[]{:S(2)}, u32[]{:S(2)}) collective-permute-start(bf16[832,384]{1,0:T(8,128)(2,1)S(1)} %constant_dynamic-update-slice_fusion.40.refs_0_), channel_id=1, source_target_pairs={{0,4},{4,0},{1,5},{5,1},{2,6},{6,2},{3,7},{7,3},{8,12},{12,8},{9,1... | collective-permute-start | bytes 1916936 | tf_op jit(solution)/shard_map/ppermute | solution.py:42
  350.6 48.3 %collective-permute-start.53 = (bf16[512,512]{1,0:T(8,128)(2,1)S(1)}, bf16[512,512]{1,0:T(8,128)(2,1)S(1)}, u32[]{:S(2)}, u32[]{:S(2)}) collective-permute-start(bf16[512,512]{1,0:T(8,128)(2,1)S(1)} %get-tuple-element.136), channel_id=1, source_target_pairs={{0,24},{8,0},{16,8},{24,16},{1,25},{9,1},{17,9},{25,17},{2,26},{10... | collective-permute-start | bytes 1572872 | tf_op jit(solution)/shard_map/ppermute | solution.py:42
  351.9 48.9 %collective-permute-start.54 = (bf16[512,512]{1,0:T(8,128)(2,1)S(1)}, bf16[512,512]{1,0:T(8,128)(2,1)S(1)}, u32[]{:S(2)}, u32[]{:S(2)}) collective-permute-start(bf16[512,512]{1,0:T(8,128)(2,1)S(1)} %get-tuple-element.137), channel_id=1, source_target_pairs={{0,16},{8,24},{16,0},{24,8},{1,17},{9,25},{17,1},{25,9},{2,18},{10... | collective-permute-start | bytes 1572872 | tf_op jit(solution)/shard_map/ppermute | solution.py:42
  354.2 49.8 %collective-permute-start.55 = (bf16[512,512]{1,0:T(8,128)(2,1)S(1)}, bf16[512,512]{1,0:T(8,128)(2,1)S(1)}, u32[]{:S(2)}, u32[]{:S(2)}) collective-permute-start(bf16[512,512]{1,0:T(8,128)(2,1)S(1)} %get-tuple-element.138), channel_id=1, source_target_pairs={{0,8},{8,16},{16,24},{24,0},{1,9},{9,17},{17,25},{25,1},{2,10},{10... | collective-permute-start | bytes 1572872 | tf_op jit(solution)/shard_map/ppermute | solution.py:42
  354.6 33.4 %collective-permute-start.75 = (bf16[512,384]{1,0:T(8,128)(2,1)S(1)}, bf16[512,384]{1,0:T(8,128)(2,1)S(1)}, u32[]{:S(2)}, u32[]{:S(2)}) collective-permute-start(bf16[512,384]{1,0:T(8,128)(2,1)S(1)} %get-tuple-element.161), channel_id=1, source_target_pairs={{0,16},{8,24},{16,0},{24,8},{1,17},{9,25},{17,1},{25,9},{2,18},{10... | collective-permute-start | bytes 1179656 | tf_op jit(solution)/shard_map/ppermute | solution.py:42
  357.9 37.3 %collective-permute-start.76 = (bf16[512,384]{1,0:T(8,128)(2,1)S(1)}, bf16[512,384]{1,0:T(8,128)(2,1)S(1)}, u32[]{:S(2)}, u32[]{:S(2)}) collective-permute-start(bf16[512,384]{1,0:T(8,128)(2,1)S(1)} %get-tuple-element.162), channel_id=1, source_target_pairs={{0,8},{8,16},{16,24},{24,0},{1,9},{9,17},{17,25},{25,1},{2,10},{10... | collective-permute-start | bytes 1179656 | tf_op jit(solution)/shard_map/ppermute | solution.py:42
  405.8 19.9 %collective-permute-start.57 = (bf16[64,512]{1,0:T(8,128)(2,1)S(1)}, bf16[64,512]{1,0:T(8,128)(2,1)S(1)}, u32[]{:S(2)}, u32[]{:S(2)}) collective-permute-start(bf16[64,512]{1,0:T(8,128)(2,1)S(1)} %get-tuple-element.141), channel_id=1, source_target_pairs={{0,192},{32,224},{64,0},{96,32},{128,64},{160,96},{192,128},{224,1... | collective-permute-start | bytes 196616 | tf_op jit(solution)/shard_map/ppermute | solution.py:42
  (70 other events, 803.1 us)

commit v3 on v2

--- a/solution.py
+++ b/solution.py
@@ -178,135 +178,231 @@
     )(*terms)
 
 
-def attend_spans(member, fetched, key_weight, value_weight, query, d_attended):
-    groups = len(fetched[0])
-    spans, piece_rows = fetched[0][0].shape[1:3]
-    here = LANES * piece_rows
-    keys = groups * here
-    features = key_weight.shape[0]
-    tokens, width = query.shape
-    heads = width // HD
-    factor = HD ** (-0.5)
-    count = len(WIDTHS) * groups
-
-    def kernel(member_ref, *refs):
-        parts = refs[:count]
-        wk_ref, wv_ref, q0_ref, q1_ref, g0_ref, g1_ref = refs[count : count + 6]
-        att_ref, dq_ref = refs[count + 6 : count + 8]
-        outs = refs[count + 8 : 2 * count + 8]
-        last_att, last_dq = refs[2 * count + 8 :]
-        span = pl.program_id(0)
-
-        @pl.when(span == 0)
-        def _():
-            last_att[...] = jnp.zeros_like(last_att)
-            last_dq[...] = jnp.zeros_like(last_dq)
-
-        def chunk_rows(chunk):
-            pieces = [
-                part[:, 0].astype(F32).reshape(here, part.shape[3])
-                for part in parts[chunk * groups : (chunk + 1) * groups]
-            ]
-            return jnp.concatenate(pieces, 0).astype(BF)
-
-        rows = jnp.concatenate([chunk_rows(chunk) for chunk in range(len(WIDTHS))], 1)
-        wk = wk_ref[...]
-        wv = wv_ref[...]
-        key_rows = matmul(rows, wk).astype(BF)
-        value_rows = matmul(rows, wv).astype(BF)
-
+def move_tokens(arrays, forward):
+    tokens, width = arrays[0].shape
+    spans = tokens // SPAN
+    count = len(arrays)
+
+    def kernel(*refs):
         to = lax.broadcasted_iota(I32, (SPAN, 2 * SPAN), 0)
         source = lax.broadcasted_iota(I32, (SPAN, 2 * SPAN), 1)
-        inside = (source < SPAN) | (span < spans - 1)
-        ahead = ((source == to + SPAN - 1) & inside).astype(F32).astype(BF)
-        back = (source == to + 1).astype(F32).astype(BF)
-        shifted = matmul(ahead, jnp.concatenate([q0_ref[...], q1_ref[...]], 0)).astype(BF)
-        grad_shift = matmul(ahead, jnp.concatenate([g0_ref[...], g1_ref[...]], 0)).astype(BF)
-
-        cols = [slice(head * HD, (head + 1) * HD) for head in range(heads)]
-        scores = [matmul(shifted[:, c], key_rows[:, c], 1, 1) * factor for c in cols]
-        grad_probs = [matmul(grad_shift[:, c], value_rows[:, c], 1, 1) for c in cols]
-        probs_b, grad_scores = [], []
-        for score, grad in zip(scores, grad_probs):
-            weights = jnp.exp(score - jnp.max(score, axis=1, keepdims=True))
-            probs = weights / jnp.sum(weights, axis=1, keepdims=True)
-            inner = jnp.sum(probs * grad, axis=1, keepdims=True)
-            probs_b.append(probs.astype(BF))
-            grad_scores.append((probs * (grad - inner) * factor).astype(BF))
-        blended = [matmul(p, value_rows[:, c]) for p, c in zip(probs_b, cols)]
-        grad_shifted = [matmul(s, key_rows[:, c]) for s, c in zip(grad_scores, cols)]
-        grad_keys = [matmul(s, shifted[:, c], 0, 0) for s, c in zip(grad_scores, cols)]
-        grad_values = [matmul(p, grad_shift[:, c], 0, 0) for p, c in zip(probs_b, cols)]
-        now_att = jnp.concatenate(blended, 1).astype(BF)
-        now_dq = jnp.concatenate(grad_shifted, 1).astype(BF)
-        att_ref[...] = matmul(back, jnp.concatenate([last_att[...], now_att], 0)).astype(BF)
-        dq_ref[...] = matmul(back, jnp.concatenate([last_dq[...], now_dq], 0)).astype(BF)
-        last_att[...] = now_att
-        last_dq[...] = now_dq
-        gk = jnp.concatenate(grad_keys, 1).astype(BF)
-        gv = jnp.concatenate(grad_values, 1).astype(BF)
-        for chunk, (start, end) in enumerate(bounds(WIDTHS)):
-            term = matmul(gk, wk[start:end], 1, 1) + matmul(gv, wv[start:end], 1, 1)
-            for group in range(groups):
-                piece = term[group * here : (group + 1) * here]
-                outs[chunk * groups + group][...] = piece.reshape(
-                    LANES, 1, piece_rows, end - start
-                ).astype(BF)
-
-    def this(i, m):
-        return (i, 0)
-
-    def following(i, m):
-        return (jnp.minimum(i + 1, spans - 1), 0)
-
-    block = (SPAN, width)
-    part_specs = [
-        pl.BlockSpec((LANES, 1, piece_rows, w), lambda i, m: (0, i, 0, 0))
-        for w in WIDTHS
-        for _ in range(groups)
+        step = SPAN - 1 if forward else 1
+        order = (source == to + step).astype(F32).astype(BF)
+        blank = jnp.zeros((SPAN, width), BF)
+        for ref, out in zip(refs[:count], refs[count:]):
+            for span in range(spans):
+                low = span if forward else span - 1
+                pair = [
+                    ref[u * SPAN : (u + 1) * SPAN] if 0 <= u < spans else blank
+                    for u in (low, low + 1)
+                ]
+                moved = matmul(order, jnp.concatenate(pair, 0))
+                out[span * SPAN : (span + 1) * SPAN] = moved.astype(BF)
+
+    return pl.pallas_call(
+        kernel,
+        out_shape=[jax.ShapeDtypeStruct((tokens, width), BF)] * count,
+        compiler_params=PARAMS,
+        cost_estimate=cost(4 * count * tokens * SPAN * width, 4 * count * tokens * width),
+        name="move_tokens",
+    )(*arrays)
+
+
+def two_heads(pair):
+    column = lax.broadcasted_iota(I32, (2 * SPAN, 2 * HD), 1)
+    row = lax.broadcasted_iota(I32, (2 * SPAN, 2 * HD), 0)
+    mask = ((column < HD) == (row < SPAN)).astype(F32).astype(BF)
+    return jnp.concatenate([pair, pair], 0) * mask
+
+
+def score_spans(fetched, key_weight, value_weight, shifted, grad_shift):
+    count = len(fetched[0])
+    chunks = len(fetched)
+    features, all_width = key_weight.shape
+    groups, tokens, width = shifted.shape
+    spans = tokens // SPAN
+    piece_rows = fetched[0][0].shape[0] // spans
+    keys = count * piece_rows
+    pairs = all_width // (2 * HD)
+    per_group = pairs // groups
+    factor = HD ** (-0.5)
+
+    def kernel(*refs):
+        wk_ref, wv_ref, q_ref, g_ref = refs[count * chunks : count * chunks + 4]
+        k_ref, v_ref, w_ref, gp_ref, stat_ref, rows_ref = refs[count * chunks + 4 :]
+
+        @pl.when(pl.program_id(0) == 0)
+        def _():
+            for chunk, (start, end) in enumerate(bounds(WIDTHS)):
+                parts = [ref[...] for ref in refs[chunk * count : (chunk + 1) * count]]
+                rows_ref[:, start:end] = jnp.concatenate(parts, 0)
+
+        rows = rows_ref[...]
+
+        def project(weight):
+            out = matmul(rows, weight).reshape(count, spans, piece_rows, 2 * HD)
+            return out.transpose(1, 0, 2, 3).reshape(spans, keys, 2 * HD).astype(BF)
+
+        k_ref[...] = project(wk_ref[...])
+        v_ref[...] = project(wv_ref[...])
+        for span in range(spans):
+            tok = pl.ds(span * SPAN, SPAN)
+            scores = matmul(k_ref[span], two_heads(q_ref[0, tok, :]), 1, 1) * factor
+            grad = matmul(v_ref[span], two_heads(g_ref[0, tok, :]), 1, 1)
+            top = jnp.max(scores, axis=0, keepdims=True)
+            weights = jnp.exp(scores - top)
+            w_ref[0, span] = weights
+            gp_ref[0, span] = grad
+            stat_ref[0, 0, pl.ds(span, 1), :] = top
+            stat_ref[0, 1, pl.ds(span, 1), :] = jnp.sum(weights, axis=0, keepdims=True)
+            stat_ref[0, 2, pl.ds(span, 1), :] = jnp.sum(weights * grad, axis=0, keepdims=True)
+
+    whole = [
+        pl.BlockSpec((spans * piece_rows, w), lambda i: (0, 0)) for w in WIDTHS for _ in range(count)
     ]
-    weight_spec = pl.BlockSpec((features, width), lambda i, m: (0, m[0]))
+    weight_spec = pl.BlockSpec((features, 2 * HD), lambda i: (0, i))
+    token_spec = pl.BlockSpec((1, tokens, 2 * HD), lambda i: (i // per_group, 0, i % per_group))
+    kv_spec = pl.BlockSpec((spans, keys, 2 * HD), lambda i: (0, 0, i))
+    score_spec = pl.BlockSpec((1, spans, keys, 2 * SPAN), lambda i: (i, 0, 0, 0))
+    return pl.pallas_call(
+        kernel,
+        grid=(pairs,),
+        in_specs=whole + [weight_spec, weight_spec, token_spec, token_spec],
+        out_specs=[
+            kv_spec,
+            kv_spec,
+            score_spec,
+            score_spec,
+            pl.BlockSpec((1, 3, spans, 2 * SPAN), lambda i: (i, 0, 0, 0)),
+        ],
+        out_shape=[
+            jax.ShapeDtypeStruct((spans, keys, all_width), BF),
+            jax.ShapeDtypeStruct((spans, keys, all_width), BF),
+            jax.ShapeDtypeStruct((pairs, spans, keys, 2 * SPAN), F32),
+            jax.ShapeDtypeStruct((pairs, spans, keys, 2 * SPAN), F32),
+            jax.ShapeDtypeStruct((pairs, 3, spans, 2 * SPAN), F32),
+        ],
+        scratch_shapes=[pltpu.VMEM((count * spans * piece_rows, features), BF)],
+        compiler_params=PARAMS,
+        cost_estimate=cost(
+            4 * spans * keys * (features + SPAN) * all_width,
+            8 * spans * keys * all_width,
+            spans * keys * SPAN * 2 * pairs,
+        ),
+        name="score_spans",
+    )(*[part for parts in fetched for part in parts], key_weight, value_weight, shifted, grad_shift)
+
+
+def blend_spans(
+    key_rows, value_rows, weights, grad_probs, stats, key_weight, value_weight, shifted, grad_shift
+):
+    features, all_width = key_weight.shape
+    groups, tokens, width = shifted.shape
+    spans, keys, _ = key_rows.shape
+    count = LANES
+    chunks = len(WIDTHS)
+    piece_rows = keys // count
+    pairs = all_width // (2 * HD)
+    per_group = pairs // groups
+    factor = HD ** (-0.5)
+    devices = len(stats)
+
+    def kernel(k_ref, v_ref, w_ref, gp_ref, *refs):
+        stat_refs = refs[:devices]
+        wk_ref, wv_ref, q_ref, g_ref, att_ref, dq_ref = refs[devices : devices + 6]
+        outs = refs[devices + 6 : devices + 6 + count * chunks]
+        total, gk_ref, gv_ref = refs[devices + 6 + count * chunks :]
+        step = pl.program_id(0)
+
+        own_top = stat_refs[0][0, 0]
+        top = own_top
+        for ref in stat_refs[1:]:
+            top = jnp.maximum(top, ref[0, 0])
+        sums = jnp.zeros_like(top)
+        inner = jnp.zeros_like(top)
+        for ref in stat_refs:
+            scale = jnp.exp(ref[0, 0] - top)
+            sums = sums + ref[0, 1] * scale
+            inner = inner + ref[0, 2] * scale
+        scale = jnp.exp(own_top - top) / sums
+        inner = inner / sums
+
+        for span in range(spans):
+            tok = pl.ds(span * SPAN, SPAN)
+            probs = w_ref[0, span] * scale[span : span + 1]
+            probs_b = probs.astype(BF)
+            grad_scores = (
+                probs * (gp_ref[0, span] - inner[span : span + 1]) * factor
+            ).astype(BF)
+            k, v = k_ref[span], v_ref[span]
+            blended = matmul(probs_b, v, 0, 0)
+            shifted_grad = matmul(grad_scores, k, 0, 0)
+            att_ref[0, tok, :HD] = blended[:SPAN, :HD].astype(BF)
+            att_ref[0, tok, HD:] = blended[SPAN:, HD:].astype(BF)
+            dq_ref[0, tok, :HD] = shifted_grad[:SPAN, :HD].astype(BF)
+            dq_ref[0, tok, HD:] = shifted_grad[SPAN:, HD:].astype(BF)
+            gk = matmul(grad_scores, two_heads(q_ref[0, tok, :]))
+            gv = matmul(probs_b, two_heads(g_ref[0, tok, :]))
+            gk_ref[:, span] = gk.reshape(count, piece_rows, 2 * HD)
+            gv_ref[:, span] = gv.reshape(count, piece_rows, 2 * HD)
+
+        flat = (count * spans * piece_rows, 2 * HD)
+        term = matmul(gk_ref[...].reshape(flat).astype(BF), wk_ref[...], 1, 1)
+        term = term + matmul(gv_ref[...].reshape(flat).astype(BF), wv_ref[...], 1, 1)
+
+        @pl.when(step == 0)
+        def _():
+            total[...] = term
+
+        @pl.when(step > 0)
+        def _():
+            total[...] += term
+
+        @pl.when(step == pairs - 1)
+        def _():
+            each = spans * piece_rows
+            for chunk, (start, end) in enumerate(bounds(WIDTHS)):
+                for part in range(count):
+                    piece = total[part * each : (part + 1) * each, start:end]
+                    outs[chunk * count + part][...] = piece.astype(BF)
+
+    weight_spec = pl.BlockSpec((features, 2 * HD), lambda i: (0, i))
+    token_spec = pl.BlockSpec((1, tokens, 2 * HD), lambda i: (i // per_group, 0, i % per_group))
+    kv_spec = pl.BlockSpec((spans, keys, 2 * HD), lambda i: (0, 0, i))
+    score_spec = pl.BlockSpec((1, spans, keys, 2 * SPAN), lambda i: (i, 0, 0, 0))
+    stat_spec = pl.BlockSpec((1, 3, spans, 2 * SPAN), lambda i: (i, 0, 0, 0))
+    parts = [(spans * piece_rows, w) for w in WIDTHS for _ in range(count)]
     outs = pl.pallas_call(
         kernel,
-        grid_spec=pltpu.PrefetchScalarGridSpec(
-            num_scalar_prefetch=1,
-            grid=(spans,),
-            in_specs=part_specs
-            + [
-                weight_spec,
-                weight_spec,
-                pl.BlockSpec(block, this),
-                pl.BlockSpec(block, following),
-                pl.BlockSpec(block, this),
-                pl.BlockSpec(block, following),
-            ],
-            out_specs=[pl.BlockSpec(block, this), pl.BlockSpec(block, this)] + part_specs,
-            scratch_shapes=[pltpu.VMEM(block, BF), pltpu.VMEM(block, BF)],
+        grid=(pairs,),
+        in_specs=[kv_spec, kv_spec, score_spec, score_spec]
+        + [stat_spec] * devices
+        + [weight_spec, weight_spec, token_spec, token_spec],
+        out_specs=[token_spec, token_spec] + [pl.BlockSpec(p, lambda i: (0, 0)) for p in parts],
+        out_shape=[jax.ShapeDtypeStruct((groups, tokens, width), BF)] * 2
+        + [jax.ShapeDtypeStruct(p, BF) for p in parts],
+        scratch_shapes=[
+            pltpu.VMEM((count * spans * piece_rows, features), F32),
+            pltpu.VMEM((count, spans, piece_rows, 2 * HD), F32),
+            pltpu.VMEM((count, spans, piece_rows, 2 * HD), F32),
+        ],
+        compiler_params=PARAMS,
+        cost_estimate=cost(
+            4 * spans * keys * (features + 2 * SPAN) * all_width, 12 * spans * keys * all_width
         ),
-        out_shape=[jax.ShapeDtypeStruct((tokens, width), BF)] * 2
-        + [
-            jax.ShapeDtypeStruct((LANES, spans, piece_rows, w), BF)
-            for w in WIDTHS
-            for _ in range(groups)
-        ],
-        compiler_params=PARAMS,
-        cost_estimate=cost(
-            spans * (8 * keys * features * width + 14 * SPAN * keys * width),
-            4 * spans * keys * features + 8 * tokens * width,
-            spans * heads * SPAN * keys,
-        ),
-        name="attend_spans",
+        name="blend_spans",
     )(
-        member,
-        *[part for parts in fetched for part in parts],
+        key_rows,
+        value_rows,
+        weights,
+        grad_probs,
+        *stats,
         key_weight,
         value_weight,
-        query,
-        query,
-        d_attended,
-        d_attended,
-    )
-    terms = [outs[2 + i * groups : 2 + (i + 1) * groups] for i in range(len(WIDTHS))]
+        shifted,
+        grad_shift,
+    )
+    terms = [outs[2 + i * count : 2 + (i + 1) * count] for i in range(chunks)]
     return outs[0], outs[1], terms
 
 
@@ -314,11 +410,15 @@
     planes = lax.axis_size("z")
     groups = lax.axis_size("x")
     columns = lax.axis_size("y")
-    z, y, c, x = [lax.axis_index(axis).astype(I32) for axis in ("z", "y", "c", "x")]
+    z, y, c = [lax.axis_index(axis).astype(I32) for axis in ("z", "y", "c")]
     spans, neighbours = nbr_shard.shape
     stored, quarter, features = encoded.shape
     rows = planes * stored * PIECE
     plane = z.reshape(1)
+
+    shifted, grad_shift = move_tokens([query, d_attended], True)
+    shifted = lax.all_gather(shifted, "x")
+    grad_shift = lax.all_gather(grad_shift, "x")
 
     own = []
     for pieces in split_pieces(encoded, plane):
@@ -338,34 +438,38 @@
     target = (first[..., None] + jnp.arange(PIECE, dtype=I32)).reshape(2, -1)
 
     fetched = []
-    for chunk, width in enumerate(WIDTHS):
-        gathered = [send_ring(own[chunk], "y", a) for a in range(columns)]
+    for piece in own:
+        gathered = [send_ring(piece, "y", a) for a in range(columns)]
         (theirs,) = pick_rows(gathered, target[1].reshape(-1, 1))
         picked = pick_rows(gathered, target[0].reshape(-1, 1), send_ring(theirs, "c", 1))
-        mine = jnp.concatenate([send_ring(part, "z", r) for r, part in enumerate(picked)], 0)
-        fetched.append(
-            [
-                send_ring(mine, "x", away).reshape(LANES, spans, neighbours * PIECE, width)
-                for away in range(groups)
-            ]
-        )
-
-    attended, d_query, terms = attend_spans(
-        x.reshape(1), fetched, key_weight, value_weight, query, d_attended
-    )
+        fetched.append([send_ring(part, "z", r) for r, part in enumerate(picked)])
+
+    key_rows, value_rows, weights, grad_probs, stats = score_spans(
+        fetched, key_weight, value_weight, shifted, grad_shift
+    )
+    stats = [send_ring(stats, "x", away) for away in range(groups)]
+    attended, d_query, terms = blend_spans(
+        key_rows,
+        value_rows,
+        weights,
+        grad_probs,
+        stats,
+        key_weight,
+        value_weight,
+        shifted,
+        grad_shift,
+    )
+    attended = lax.psum_scatter(attended, "x", scatter_dimension=0)
+    d_query = lax.psum_scatter(d_query, "x", scatter_dimension=0)
 
     returned = []
-    for chunk, parts in enumerate(terms):
-        width = WIDTHS[chunk]
-        arrived = [
-            send_ring(part.reshape(-1, width), "x", -away) for away, part in enumerate(parts)
-        ]
-        d_nbr = add_and_cut(arrived, planes)
-        home = jnp.concatenate([send_ring(part, "z", -r) for r, part in enumerate(d_nbr)], 0)
+    for parts in terms:
+        home = jnp.concatenate([send_ring(part, "z", -r) for r, part in enumerate(parts)], 0)
         sums = sum_rows([home, send_ring(home, "c", 1)], target.reshape(1, -1), columns, rows)
         whole = add_and_cut([send_ring(part, "y", -a) for a, part in enumerate(sums)], planes)
         returned.append([send_ring(part, "z", -k) for k, part in enumerate(whole)])
     d_encoded = join_pieces(returned, plane, stored, quarter, features)
+    attended, d_query = move_tokens([attended, d_query], False)
     return (attended, d_query, d_encoded)
 
 

time: 443 us -> 372 us (0.84)
  waiting for transfers between devices: 184 us -> 113 us
  starting transfers between devices: 167 us -> 147 us
  between operations: 2.22 us -> 15.3 us
  Pallas kernels: 54.3 us -> 63.3 us
    ppermute x84 -> x75, waiting for transfers between devices: 184 us -> 112 us  [send_ring(): lax.ppermute(array, axis, [(i, (i + step) % size) for i in range(size)])]
    ppermute x84 -> x75, starting transfers between devices: 167 us -> 147 us  [send_ring(): lax.ppermute(array, axis, [(i, (i + step) % size) for i in range(size)])]
    pallas_call x1 -> x4, Pallas kernels: 32.2 us -> 41.3 us  [the longest x1 20.8 us: blend_spans(): pl.pallas_call(kernel, grid=(pairs,), in_specs=[kv_spec, kv_spec, score_s...]
    unnamed x65 -> x69, local copies, waits for them, and re-layouts: 10.7 us -> 11.1 us
  transfers between devices with their start and end apart: 84 -> 79, of which waited for: 35 -> 34; matrix products, arithmetic and copies ran while one was open for 2% -> 1% of each run, Pallas kernels for 5% -> 6%
where the time goes in v3:
time: 372 us; the launch traced here: 365 us
  starting transfers between devices  147 us (40%)
  waiting for transfers between devices  113 us (30%)
  Pallas kernels  63.3 us (17%)
  between operations  15.3 us (4%)
  local copies, waits for them, and re-layouts  13.4 us (4%)
  blocking collectives  12.4 us (3%)
    ppermute x75, starting transfers between devices, send_ring(): lax.ppermute(array, axis, [(i, (i + step) % size) for i in range(size)])  147 us
    ppermute x75, waiting for transfers between devices, send_ring(): lax.ppermute(array, axis, [(i, (i + step) % size) for i in range(size)])  112 us
    pallas_call x1, Pallas kernels, blend_spans(): pl.pallas_call(kernel, grid=(pairs,), in_specs=[kv_spec, kv_spec, score_s...  20.8 us
    pallas_call x1, Pallas kernels, score_spans(): pl.pallas_call(kernel, grid=(pairs,), in_specs=whole + [weight_spec, weig...  17.2 us
    unnamed x1, blocking collectives  12.4 us
    pallas_call x4, Pallas kernels, pick_rows(): pl.pallas_call(kernel, out_shape=[jax.ShapeDtypeStruct((each, width), BF)...  11.3 us
    unnamed x69, local copies, waits for them, and re-layouts  11.1 us
    pallas_call x2, Pallas kernels, sum_rows(): pl.pallas_call(kernel, out_shape=[jax.ShapeDtypeStruct((rows, width), BF)...  7.78 us
  transfers between devices with their start and end apart: 79, of which 34 were waited for; matrix products, arithmetic and copies ran while one was open for 1% of the time, Pallas kernels for 6%

profile of v3, /device:TPU:16, one launch (start us, length us, event | category | flops | bytes accessed | tf_op | source)
XLA Modules:
  0.0 364.8 jit_solution(1444639592760534866)
XLA Ops:
  18.0 4.0 %collective-permute-start.20 = (bf16[64,384]{1,0:T(8,128)(2,1)S(1)}, bf16[64,384]{1,0:T(8,128)(2,1)S(1)}, u32[]{:S(2)}, u32[]{:S(2)}) collective-permute-start(bf16[64,384]{1,0:T(8,128)(2,1)S(1)} %get-tuple-element.109), channel_id=1, source_target_pairs={{0,96},{32,128},{64,160},{96,192},{128,224},{160,0},{192,32},{224,... | collective-permute-start | bytes 147464 | tf_op jit(solution)/shard_map/ppermute | solution.py:42
  22.6 5.0 %collective-permute-start.22 = (bf16[64,384]{1,0:T(8,128)(2,1)S(1)}, bf16[64,384]{1,0:T(8,128)(2,1)S(1)}, u32[]{:S(2)}, u32[]{:S(2)}) collective-permute-start(bf16[64,384]{1,0:T(8,128)(2,1)S(1)} %get-tuple-element.111), channel_id=1, source_target_pairs={{0,160},{32,192},{64,224},{96,0},{128,32},{160,64},{192,96},{224,1... | collective-permute-start | bytes 147464 | tf_op jit(solution)/shard_map/ppermute | solution.py:42
  36.6 3.7 %collective-permute-start.3 = (bf16[64,512]{1,0:T(8,128)(2,1)S(1)}, bf16[64,512]{1,0:T(8,128)(2,1)S(1)}, u32[]{:S(2)}, u32[]{:S(2)}) collective-permute-start(bf16[64,512]{1,0:T(8,128)(2,1)S(1)} %get-tuple-element.92), channel_id=1, source_target_pairs={{0,128},{32,160},{64,192},{96,224},{128,0},{160,32},{192,64},{224,... | collective-permute-start | bytes 196616 | tf_op jit(solution)/shard_map/ppermute | solution.py:42
  59.0 12.4 %all-reduce = s32[416]{0:T(512)S(1)} all-reduce(s32[416]{0:T(512)S(1)} %dynamic-update-slice), channel_id=1, replica_groups=mesh['z'=8,'y'=4,'c'=2,'x'=4] {'z','c'}, use_global_device_ids=true, to_apply=%add | all-reduce | flops 416 | bytes 3328
  79.4 9.6 %collective-permute-done.7.refs_1_ = bf16[512,512]{1,0:T(8,128)(2,1)S(1)} collective-permute-done((bf16[512,512]{1,0:T(8,128)(2,1)S(1)}, bf16[512,512]{1,0:T(8,128)(2,1)S(1)}, u32[]{:S(2)}, u32[]{:S(2)}) %collective-permute-start.7) | collective-permute-done | bytes 524320 | tf_op jit(solution)/shard_map/ppermute | solution.py:42
  94.9 4.0 %pick_rows.6 = bf16[832,384]{1,0:T(8,128)(2,1)} custom-call(s32[832,1]{1,0:T(8,128)S(1)} %reshape_squeeze.11.target_ref, bf16[512,384]{1,0:T(8,128)(2,1)S(1)} %constant_dynamic-update-slice_fusion.8.refs_0_, bf16[512,384]{1,0:T(8,128)(2,1)} %collective-permute-done.25.refs_1_, bf16[512,384]{1,0:T(8,128)(2,1)} %collective-permute-done.26.refs_2_, ...), custom_call_target="tpu_custom_call" | custom-call | flops 1308622848 | bytes 2211840 | tf_op jit(solution)/shard_map/pick_rows/pallas_call | solution.py:126
  109.1 8.8 %collective-permute-start.31 = (bf16[104,384]{1,0:T(8,128)(2,1)S(1)}, bf16[104,384]{1,0:T(8,128)(2,1)S(1)}, u32[]{:S(2)}, u32[]{:S(2)}) collective-permute-start(bf16[104,384]{1,0:T(8,128)(2,1)S(1)} %get-tuple-element.117), channel_id=1, source_target_pairs={{0,96},{32,128},{64,160},{96,192},{128,224},{160,0},{192,32},{224,... | collective-permute-start | bytes 239624 | tf_op jit(solution)/shard_map/ppermute | solution.py:42
  139.4 3.7 %collective-permute-start.14 = (bf16[104,512]{1,0:T(8,128)(2,1)S(1)}, bf16[104,512]{1,0:T(8,128)(2,1)S(1)}, u32[]{:S(2)}, u32[]{:S(2)}) collective-permute-start(bf16[104,512]{1,0:T(8,128)(2,1)S(1)} %get-tuple-element.102), channel_id=1, source_target_pairs={{0,128},{32,160},{64,192},{96,224},{128,0},{160,32},{192,64},{224,... | collective-permute-start | bytes 319496 | tf_op jit(solution)/shard_map/ppermute | solution.py:42
  143.8 4.6 %collective-permute-start.16 = (bf16[104,512]{1,0:T(8,128)(2,1)S(1)}, bf16[104,512]{1,0:T(8,128)(2,1)S(1)}, u32[]{:S(2)}, u32[]{:S(2)}) collective-permute-start(bf16[104,512]{1,0:T(8,128)(2,1)S(1)} %get-tuple-element.104), channel_id=1, source_target_pairs={{0,192},{32,224},{64,0},{96,32},{128,64},{160,96},{192,128},{224,1... | collective-permute-start | bytes 319496 | tf_op jit(solution)/shard_map/ppermute | solution.py:42
  150.4 6.8 %collective-permute-done.15.refs_5_ = bf16[104,512]{1,0:T(8,128)(2,1)S(1)} collective-permute-done((bf16[104,512]{1,0:T(8,128)(2,1)S(1)}, bf16[104,512]{1,0:T(8,128)(2,1)S(1)}, u32[]{:S(2)}, u32[]{:S(2)}) %collective-permute-start.15) | collective-permute-done | bytes 106528 | tf_op jit(solution)/shard_map/ppermute | solution.py:42
  160.8 17.2 %score_spans.1 = (bf16[13,64,2048]{2,1,0:T(8,128)(2,1)S(1)}, bf16[13,64,2048]{2,1,0:T(8,128)(2,1)}, f32[8,13,64,128]{3,2,1,0:T(8,128)}, f32[8,13,64,128]{3,2,1,0:T(8,128)}, f32[8,3,13,128]{3,2,1,0:T(8,128)S(1)}) custom-call(bf16[104,512]{1,0:T(8,128)(2,1)S(1)} %get-tuple-element.98.refs_0_, bf16[104,512]{1,0:T(8,128)(2,1)S(1)} %collective-permute-done.11.refs_1_, ...), custom_call_target="tpu_custom_call" | custom-call | flops 6543114240 | bytes 13631488 | tf_op jit(solution)/shard_map/score_spans/pallas_call | solution.py:267
  184.2 5.4 %collective-permute-done.38.refs_3_ = f32[8,3,13,128]{3,2,1,0:T(8,128)S(1)} collective-permute-done((f32[8,3,13,128]{3,2,1,0:T(8,128)S(1)}, f32[8,3,13,128]{3,2,1,0:T(8,128)S(1)}, u32[]{:S(2)}, u32[]{:S(2)}) %collective-permute-start.38) | collective-permute-done | bytes 159776 | tf_op jit(solution)/shard_map/ppermute | solution.py:42
  193.2 20.8 %blend_spans.1 = (bf16[4,832,512]{2,1,0:T(8,128)(2,1)}, bf16[4,832,512]{2,1,0:T(8,128)(2,1)}, bf16[104,512]{1,0:T(8,128)(2,1)S(1)}, bf16[104,512]{1,0:T(8,128)(2...) custom-call(bf16[13,64,2048]{2,1,0:T(8,128)(2,1)} %copy-done, ...), custom_call_target="tpu_custom_call" | custom-call | flops 6979321856 | bytes 20447232 | tf_op jit(solution)/shard_map/blend_spans/pallas_call | solution.py:375
  219.4 4.6 %collective-permute-start.60 = (bf16[104,384]{1,0:T(8,128)(2,1)S(1)}, bf16[104,384]{1,0:T(8,128)(2,1)S(1)}, u32[]{:S(2)}, u32[]{:S(2)}) collective-permute-start(bf16[104,384]{1,0:T(8,128)(2,1)S(1)} %get-tuple-element.157), channel_id=1, source_target_pairs={{0,128},{32,160},{64,192},{96,224},{128,0},{160,32},{192,64},{224,... | collective-permute-start | bytes 239624 | tf_op jit(solution)/shard_map/ppermute | solution.py:42
  233.1 4.9 %collective-permute-start.40 = (bf16[104,512]{1,0:T(8,128)(2,1)S(1)}, bf16[104,512]{1,0:T(8,128)(2,1)S(1)}, u32[]{:S(2)}, u32[]{:S(2)}) collective-permute-start(bf16[104,512]{1,0:T(8,128)(2,1)S(1)} %get-tuple-element.135), channel_id=1, source_target_pairs={{0,192},{32,224},{64,0},{96,32},{128,64},{160,96},{192,128},{224,1... | collective-permute-start | bytes 319496 | tf_op jit(solution)/shard_map/ppermute | solution.py:42
  238.1 3.8 %collective-permute-start.42 = (bf16[104,512]{1,0:T(8,128)(2,1)S(1)}, bf16[104,512]{1,0:T(8,128)(2,1)S(1)}, u32[]{:S(2)}, u32[]{:S(2)}) collective-permute-start(bf16[104,512]{1,0:T(8,128)(2,1)S(1)} %get-tuple-element.137), channel_id=1, source_target_pairs={{0,128},{32,160},{64,192},{96,224},{128,0},{160,32},{192,64},{224,... | collective-permute-start | bytes 319496 | tf_op jit(solution)/shard_map/ppermute | solution.py:42
  242.3 4.0 %collective-permute-start.44 = (bf16[104,512]{1,0:T(8,128)(2,1)S(1)}, bf16[104,512]{1,0:T(8,128)(2,1)S(1)}, u32[]{:S(2)}, u32[]{:S(2)}) collective-permute-start(bf16[104,512]{1,0:T(8,128)(2,1)S(1)} %get-tuple-element.139), channel_id=1, source_target_pairs={{0,64},{32,96},{64,128},{96,160},{128,192},{160,224},{192,0},{224,... | collective-permute-start | bytes 319496 | tf_op jit(solution)/shard_map/ppermute | solution.py:42
  250.8 5.1 %collective-permute-done.43 = bf16[104,512]{1,0:T(8,128)(2,1)S(1)} collective-permute-done((bf16[104,512]{1,0:T(8,128)(2,1)S(1)}, bf16[104,512]{1,0:T(8,128)(2,1)S(1)}, u32[]{:S(2)}, u32[]{:S(2)}) %collective-permute-start.43) | collective-permute-done | bytes 106528 | tf_op jit(solution)/shard_map/ppermute | solution.py:42
  260.8 3.8 %sum_rows.3 = (bf16[512,384]{1,0:T(8,128)(2,1)S(1)}, bf16[512,384]{1,0:T(8,128)(2,1)S(1)}, bf16[512,384]{1,0:T(8,128)(2,1)S(1)}, bf16[512,384]{1,0:T(8,128)(2,1)S(1)}) custom-call(s32[1,1664]{1,0:T(1,128)S(1)} %add.95.target_ref, bf16[832,384]{1,0:T(8,128)(2,1)S(1)} %constant_dynamic-update-slice_fusion.24.refs_0_, ...), custom_call_target="tpu_custom_call" | custom-call | flops 2617245696 | bytes 2850816 | tf_op jit(solution)/shard_map/sum_rows/pallas_call | solution.py:149
  264.7 3.8 %collective-permute-start.65 = (bf16[512,384]{1,0:T(8,128)(2,1)S(1)}, bf16[512,384]{1,0:T(8,128)(2,1)S(1)}, u32[]{:S(2)}, u32[]{:S(2)}) collective-permute-start(bf16[512,384]{1,0:T(8,128)(2,1)S(1)} %get-tuple-element.162), channel_id=1, source_target_pairs={{0,24},{8,0},{16,8},{24,16},{1,25},{9,1},{17,9},{25,17},{2,26},{10... | collective-permute-start | bytes 1179656 | tf_op jit(solution)/shard_map/ppermute | solution.py:42
  268.5 3.9 %sum_rows.2 = (bf16[512,512]{1,0:T(8,128)(2,1)S(1)}, bf16[512,512]{1,0:T(8,128)(2,1)S(1)}, bf16[512,512]{1,0:T(8,128)(2,1)S(1)}, bf16[512,512]{1,0:T(8,128)(2,1)S(1)}) custom-call(s32[1,1664]{1,0:T(1,128)S(1)} %add.95.target_ref, bf16[832,512]{1,0:T(8,128)(2,1)S(1)} %constant_dynamic-update-slice_fusion.16.refs_0_, ...), custom_call_target="tpu_custom_call" | custom-call | flops 3489660928 | bytes 3801088 | tf_op jit(solution)/shard_map/sum_rows/pallas_call | solution.py:149
  282.1 26.6 %collective-permute-done.66.refs_2_ = bf16[512,384]{1,0:T(8,128)(2,1)S(1)} collective-permute-done((bf16[512,384]{1,0:T(8,128)(2,1)S(1)}, bf16[512,384]{1,0:T(8,128)(2,1)S(1)}, u32[]{:S(2)}, u32[]{:S(2)}) %collective-permute-start.66) | collective-permute-done | bytes 393248 | tf_op jit(solution)/shard_map/ppermute | solution.py:42
  308.7 7.5 %collective-permute-done.67.refs_3_ = bf16[512,384]{1,0:T(8,128)(2,1)S(1)} collective-permute-done((bf16[512,384]{1,0:T(8,128)(2,1)S(1)}, bf16[512,384]{1,0:T(8,128)(2,1)S(1)}, u32[]{:S(2)}, u32[]{:S(2)}) %collective-permute-start.67) | collective-permute-done | bytes 393248 | tf_op jit(solution)/shard_map/ppermute | solution.py:42
  332.3 3.9 %collective-permute-done.72.refs_13_ = bf16[64,384]{1,0:T(8,128)(2,1)S(1)} collective-permute-done((bf16[64,384]{1,0:T(8,128)(2,1)S(1)}, bf16[64,384]{1,0:T(8,128)(2,1)S(1)}, u32[]{:S(2)}, u32[]{:S(2)}) %collective-permute-start.72) | collective-permute-done | bytes 49184 | tf_op jit(solution)/shard_map/ppermute | solution.py:42
  (238 shorter events, 171.7 us)
Async XLA Ops:
  7.2 153.7 %all-gather.5.cloned.1.call-start = ((), (), s32[]{:S(2)}) async-start(), calls=%async_computation.4 | async-start | bytes 4259840 | tf_op jit(solution)/shard_map/all_gather | solution.py:420
  11.2 149.6 %all-gather.7.cloned.1.call-start = ((), (), s32[]{:S(2)}) async-start(), calls=%async_computation.5 | async-start | bytes 4259840 | tf_op jit(solution)/shard_map/all_gather | solution.py:421
  11.9 342.1 %reduce-scatter.3.cloned.1.call-start = ((), (), s32[]{:S(2)}) async-start(), calls=%async_computation.2 | async-start | bytes 4259840 | tf_op jit(solution)/shard_map/reduce_scatter | solution.py:462
  31.9 21.3 %collective-permute-start.24 = (bf16[64,384]{1,0:T(8,128)(2,1)S(1)}, bf16[64,384]{1,0:T(8,128)(2,1)S(1)}, u32[]{:S(2)}, u32[]{:S(2)}) collective-permute-start(bf16[64,384]{1,0:T(8,128)(2,1)S(1)} %get-tuple-element.113), channel_id=1, source_target_pairs={{0,224},{32,0},{64,32},{96,64},{128,96},{160,128},{192,160},{224,1... | collective-permute-start | bytes 147464 | tf_op jit(solution)/shard_map/ppermute | solution.py:42
  52.4 19.4 %collective-permute-start.9 = (bf16[512,512]{1,0:T(8,128)(2,1)S(1)}, bf16[512,512]{1,0:T(8,128)(2,1)S(1)}, u32[]{:S(2)}, u32[]{:S(2)}) collective-permute-start(bf16[512,512]{1,0:T(8,128)(2,1)S(1)} %constant_dynamic-update-slice_fusion.refs_0_), channel_id=1, source_target_pairs={{0,24},{8,0},{16,8},{24,16},{1,25},{9,1},{17,9},{25,17},{2,26},{10... | collective-permute-start | bytes 1572872 | tf_op jit(solution)/shard_map/ppermute | solution.py:42
  53.1 40.8 %collective-permute-start.27 = (bf16[512,384]{1,0:T(8,128)(2,1)S(1)}, bf16[512,384]{1,0:T(8,128)(2,1)S(1)}, u32[]{:S(2)}, u32[]{:S(2)}) collective-permute-start(bf16[512,384]{1,0:T(8,128)(2,1)S(1)} %constant_dynamic-update-slice_fusion.8.refs_0_), channel_id=1, source_target_pairs={{0,24},{8,0},{16,8},{24,16},{1,25},{9,1},{17,9},{25,17},{2,26},{10... | collective-permute-start | bytes 1179656 | tf_op jit(solution)/shard_map/ppermute | solution.py:42
  53.7 40.3 %collective-permute-start.26 = (bf16[512,384]{1,0:T(8,128)(2,1)S(1)}, bf16[512,384]{1,0:T(8,128)(2,1)}, u32[]{:S(2)}, u32[]{:S(2)}) collective-permute-start(bf16[512,384]{1,0:T(8,128)(2,1)S(1)} %constant_dynamic-update-slice_fusion.8.refs_0_), channel_id=1, source_target_pairs={{0,16},{8,24},{16,0},{24,8},{1,17},{9,25},{17,1},{25,9},{2,18},{10... | collective-permute-start | bytes 1179656 | tf_op jit(solution)/shard_map/ppermute | solution.py:42
  56.9 21.7 %collective-permute-start.8 = (bf16[512,512]{1,0:T(8,128)(2,1)S(1)}, bf16[512,512]{1,0:T(8,128)(2,1)S(1)}, u32[]{:S(2)}, u32[]{:S(2)}) collective-permute-start(bf16[512,512]{1,0:T(8,128)(2,1)S(1)} %constant_dynamic-update-slice_fusion.refs_0_), channel_id=1, source_target_pairs={{0,16},{8,24},{16,0},{24,8},{1,17},{9,25},{17,1},{25,9},{2,18},{10... | collective-permute-start | bytes 1572872 | tf_op jit(solution)/shard_map/ppermute | solution.py:42
  57.2 31.7 %collective-permute-start.7 = (bf16[512,512]{1,0:T(8,128)(2,1)S(1)}, bf16[512,512]{1,0:T(8,128)(2,1)S(1)}, u32[]{:S(2)}, u32[]{:S(2)}) collective-permute-start(bf16[512,512]{1,0:T(8,128)(2,1)S(1)} %constant_dynamic-update-slice_fusion.refs_0_), channel_id=1, source_target_pairs={{0,8},{8,16},{16,24},{24,0},{1,9},{9,17},{17,25},{25,1},{2,10},{10... | collective-permute-start | bytes 1572872 | tf_op jit(solution)/shard_map/ppermute | solution.py:42
  71.8 23.1 %collective-permute-start.25 = (bf16[512,384]{1,0:T(8,128)(2,1)S(1)}, bf16[512,384]{1,0:T(8,128)(2,1)}, u32[]{:S(2)}, u32[]{:S(2)}) collective-permute-start(bf16[512,384]{1,0:T(8,128)(2,1)S(1)} %constant_dynamic-update-slice_fusion.8.refs_0_), channel_id=1, source_target_pairs={{0,8},{8,16},{16,24},{24,0},{1,9},{9,17},{17,25},{25,1},{2,10},{10... | collective-permute-start | bytes 1179656 | tf_op jit(solution)/shard_map/ppermute | solution.py:42
  93.9 27.4 %collective-permute-start.10 = (bf16[832,512]{1,0:T(8,128)(2,1)S(1)}, bf16[832,512]{1,0:T(8,128)(2,1)S(1)}, u32[]{:S(2)}, u32[]{:S(2)}) collective-permute-start(bf16[832,512]{1,0:T(8,128)(2,1)S(1)} %pick_rows.4), channel_id=1, source_target_pairs={{0,4},{4,0},{1,5},{5,1},{2,6},{6,2},{3,7},{7,3},{8,12},{12,8},{9,1... | collective-permute-start | bytes 2555912 | tf_op jit(solution)/shard_map/ppermute | solution.py:42
  104.6 21.8 %collective-permute-start.29 = (bf16[104,384]{1,0:T(8,128)(2,1)S(1)}, bf16[104,384]{1,0:T(8,128)(2,1)S(1)}, u32[]{:S(2)}, u32[]{:S(2)}) collective-permute-start(bf16[104,384]{1,0:T(8,128)(2,1)S(1)} %get-tuple-element.115), channel_id=1, source_target_pairs={{0,32},{32,64},{64,96},{96,128},{128,160},{160,192},{192,224},{224... | collective-permute-start | bytes 239624 | tf_op jit(solution)/shard_map/ppermute | solution.py:42
  106.0 21.0 %collective-permute-start.30 = (bf16[104,384]{1,0:T(8,128)(2,1)S(1)}, bf16[104,384]{1,0:T(8,128)(2,1)S(1)}, u32[]{:S(2)}, u32[]{:S(2)}) collective-permute-start(bf16[104,384]{1,0:T(8,128)(2,1)S(1)} %get-tuple-element.116), channel_id=1, source_target_pairs={{0,64},{32,96},{64,128},{96,160},{128,192},{160,224},{192,0},{224,... | collective-permute-start | bytes 239624 | tf_op jit(solution)/shard_map/ppermute | solution.py:42
  109.1 21.5 %collective-permute-start.31 = (bf16[104,384]{1,0:T(8,128)(2,1)S(1)}, bf16[104,384]{1,0:T(8,128)(2,1)S(1)}, u32[]{:S(2)}, u32[]{:S(2)}) collective-permute-start(bf16[104,384]{1,0:T(8,128)(2,1)S(1)} %get-tuple-element.117), channel_id=1, source_target_pairs={{0,96},{32,128},{64,160},{96,192},{128,224},{160,0},{192,32},{224,... | collective-permute-start | bytes 239624 | tf_op jit(solution)/shard_map/ppermute | solution.py:42
  123.3 20.5 %collective-permute-start.11 = (bf16[104,512]{1,0:T(8,128)(2,1)S(1)}, bf16[104,512]{1,0:T(8,128)(2,1)S(1)}, u32[]{:S(2)}, u32[]{:S(2)}) collective-permute-start(bf16[104,512]{1,0:T(8,128)(2,1)S(1)} %get-tuple-element.99), channel_id=1, source_target_pairs={{0,32},{32,64},{64,96},{96,128},{128,160},{160,192},{192,224},{224... | collective-permute-start | bytes 319496 | tf_op jit(solution)/shard_map/ppermute | solution.py:42
  126.4 22.0 %collective-permute-start.12 = (bf16[104,512]{1,0:T(8,128)(2,1)S(1)}, bf16[104,512]{1,0:T(8,128)(2,1)S(1)}, u32[]{:S(2)}, u32[]{:S(2)}) collective-permute-start(bf16[104,512]{1,0:T(8,128)(2,1)S(1)} %get-tuple-element.100), channel_id=1, source_target_pairs={{0,64},{32,96},{64,128},{96,160},{128,192},{160,224},{192,0},{224,... | collective-permute-start | bytes 319496 | tf_op jit(solution)/shard_map/ppermute | solution.py:42
  214.1 140.0 %reduce-scatter.5.cloned.1.call-start = ((), (), s32[]{:S(2)}) async-start(), calls=%async_computation.3 | async-start | bytes 4259840 | tf_op jit(solution)/shard_map/reduce_scatter | solution.py:463
  272.4 47.1 %collective-permute-start.47 = (bf16[512,512]{1,0:T(8,128)(2,1)S(1)}, bf16[512,512]{1,0:T(8,128)(2,1)S(1)}, u32[]{:S(2)}, u32[]{:S(2)}) collective-permute-start(bf16[512,512]{1,0:T(8,128)(2,1)S(1)} %get-tuple-element.142), channel_id=1, source_target_pairs={{0,24},{8,0},{16,8},{24,16},{1,25},{9,1},{17,9},{25,17},{2,26},{10... | collective-permute-start | bytes 1572872 | tf_op jit(solution)/shard_map/ppermute | solution.py:42
  272.7 49.1 %collective-permute-start.48 = (bf16[512,512]{1,0:T(8,128)(2,1)S(1)}, bf16[512,512]{1,0:T(8,128)(2,1)S(1)}, u32[]{:S(2)}, u32[]{:S(2)}) collective-permute-start(bf16[512,512]{1,0:T(8,128)(2,1)S(1)} %get-tuple-element.143), channel_id=1, source_target_pairs={{0,16},{8,24},{16,0},{24,8},{1,17},{9,25},{17,1},{25,9},{2,18},{10... | collective-permute-start | bytes 1572872 | tf_op jit(solution)/shard_map/ppermute | solution.py:42
  275.0 49.3 %collective-permute-start.49 = (bf16[512,512]{1,0:T(8,128)(2,1)S(1)}, bf16[512,512]{1,0:T(8,128)(2,1)S(1)}, u32[]{:S(2)}, u32[]{:S(2)}) collective-permute-start(bf16[512,512]{1,0:T(8,128)(2,1)S(1)} %get-tuple-element.144), channel_id=1, source_target_pairs={{0,8},{8,16},{16,24},{24,0},{1,9},{9,17},{17,25},{25,1},{2,10},{10... | collective-permute-start | bytes 1572872 | tf_op jit(solution)/shard_map/ppermute | solution.py:42
  277.5 31.2 %collective-permute-start.66 = (bf16[512,384]{1,0:T(8,128)(2,1)S(1)}, bf16[512,384]{1,0:T(8,128)(2,1)S(1)}, u32[]{:S(2)}, u32[]{:S(2)}) collective-permute-start(bf16[512,384]{1,0:T(8,128)(2,1)S(1)} %get-tuple-element.163), channel_id=1, source_target_pairs={{0,16},{8,24},{16,0},{24,8},{1,17},{9,25},{17,1},{25,9},{2,18},{10... | collective-permute-start | bytes 1179656 | tf_op jit(solution)/shard_map/ppermute | solution.py:42
  278.8 37.5 %collective-permute-start.67 = (bf16[512,384]{1,0:T(8,128)(2,1)S(1)}, bf16[512,384]{1,0:T(8,128)(2,1)S(1)}, u32[]{:S(2)}, u32[]{:S(2)}) collective-permute-start(bf16[512,384]{1,0:T(8,128)(2,1)S(1)} %get-tuple-element.164), channel_id=1, source_target_pairs={{0,8},{8,16},{16,24},{24,0},{1,9},{9,17},{17,25},{25,1},{2,10},{10... | collective-permute-start | bytes 1179656 | tf_op jit(solution)/shard_map/ppermute | solution.py:42
  324.6 18.2 %collective-permute-start.50 = (bf16[64,512]{1,0:T(8,128)(2,1)S(1)}, bf16[64,512]{1,0:T(8,128)(2,1)S(1)}, u32[]{:S(2)}, u32[]{:S(2)}) collective-permute-start(bf16[64,512]{1,0:T(8,128)(2,1)S(1)} %get-tuple-element.146), channel_id=1, source_target_pairs={{0,224},{32,0},{64,32},{96,64},{128,96},{160,128},{192,160},{224,1... | collective-permute-start | bytes 196616 | tf_op jit(solution)/shard_map/ppermute | solution.py:42
  326.3 18.7 %collective-permute-start.51 = (bf16[64,512]{1,0:T(8,128)(2,1)S(1)}, bf16[64,512]{1,0:T(8,128)(2,1)S(1)}, u32[]{:S(2)}, u32[]{:S(2)}) collective-permute-start(bf16[64,512]{1,0:T(8,128)(2,1)S(1)} %get-tuple-element.147), channel_id=1, source_target_pairs={{0,192},{32,224},{64,0},{96,32},{128,64},{160,96},{192,128},{224,1... | collective-permute-start | bytes 196616 | tf_op jit(solution)/shard_map/ppermute | solution.py:42
  (74 other events, 807.9 us)
Sparse Core Ops, SparseCore 0:
  11.3 47.0 all-gather.4
  60.8 44.5 all-gather.6
  214.2 42.8 reduce-scatter.2
  259.5 42.6 reduce-scatter.4
